TPU v7x, 512 devices: a whole 4x4x16 slice. The times are simulated.
512 devices in a mesh: dom: 128 (over z, x, core), ray: 4 (over y).
Axes of the slice: x: 4, y: 4, z: 16, core: 2. Of those that a mesh axis runs over, the one named last changes fastest.
Arguments:
- anchor: float32 [3, 4, 512], P(None, 'ray'), may hold values from -4 to 4
- direct: float32 [3, 4, 512], P(None, 'ray'), may hold values from -3 to 3
- entry: float32 [4, 512, 4], P('ray'), may hold values from 0 to 2
- step: float32 [4, 512, 4], P('ray'), may hold values from 0.004 to 0.04
- counts: int32 [4, 512, 4], P('ray'), may hold values from 1 to 64
- crossing: int32 [4, 512, 4], P('ray'), may hold values from 0 to 127, all different within a row; in each aligned block of 512 rows (0 to 511, 512 to 1023, ..., all dimensions but the last counted through in order) at most 64 rows name the same one
- order: int32 [4, 8, 128], P('ray'), may hold values from 0 to 127, each once within a row
- target: float32 [3, 4, 512], P(None, 'ray'), may hold values from 0 to 1
- w_in: bfloat16 [128, 256, 63], P('dom'), may hold values from -0.75 to 0.75
- w_mid: bfloat16 [128, 256, 256], P('dom'), may hold values from -0.5 to 0.5
- w_out: bfloat16 [128, 4, 256], P('dom'), may hold values from -0.5 to 0.5
Outputs:
- rendered: float32 [3, 4, 512], P(None, 'ray', 'dom')
- grad_in: float32 [128, 256, 63], P('dom')
- grad_mid: float32 [128, 256, 256], P('dom')
- grad_out: float32 [128, 4, 256], P('dom')
Inputs may be any that keep to these rules, and one draw needn't show every extreme that they name: `crossing`: each ray names 4 different partitions; among the rays of one group no partition is named by more than 64 rays, and one is named by exactly 64. `order`: each bundle's row names every partition once.
All inputs are finite; a program needn't handle non-finite values.
Results may differ from a plain program's by a relative error of at most 0.024.
Values sent between devices are 32-bit elements; how exact they have to be, the bound alone decides.
No kernel may reach another device: no remote copies, remote signals or barrier semaphores. Data moves between devices by JAX's collectives and lax.ppermute only.
A program may use at most 64 MiB of HBM per device.

v0:
```python
import jax
import jax.numpy as jnp
from jax import lax
from jax.sharding import PartitionSpec as P

NFREQ = 10
S = 64
K = 4
NB = 8
RAYS_DEV = 4


def slot_inputs(crossings, partition, anchor_g, direct_g, entry_g, step_g, counts_g, capacity):
    hit_mask = crossings == partition
    crossed = jnp.any(hit_mask, axis=1)
    places = jnp.cumsum(crossed.astype(jnp.int32)) - 1
    slot_ids = jnp.arange(capacity, dtype=jnp.int32)
    selector = jnp.logical_and(places[None, :] == slot_ids[:, None], crossed[None, :])
    hit_float = hit_mask.astype(jnp.float32)
    selector_f = selector.astype(jnp.float32)
    entry_ray = jnp.sum(hit_float * entry_g, axis=1)
    step_ray = jnp.sum(hit_float * step_g, axis=1)
    count_ray = jnp.sum(jnp.where(hit_mask, counts_g, 0), axis=1)

    def picked(values):
        return jnp.dot(
            values,
            selector_f.T,
            precision=lax.Precision.HIGHEST,
            preferred_element_type=jnp.float32,
        )

    anchor_s = picked(anchor_g)
    direct_s = picked(direct_g)
    entry_s = picked(entry_ray[None, :])[0]
    step_s = picked(step_ray[None, :])[0]
    count_s = jnp.sum(jnp.where(selector, count_ray[None, :], 0), axis=1)
    return (selector_f, anchor_s, direct_s, entry_s, step_s, count_s)


def encode_points(anchor_s, direct_s, entry_s, step_s):
    offsets = jnp.arange(S, dtype=jnp.float32) + 0.5
    depths = entry_s[:, None] + offsets[None, :] * step_s[:, None]
    points = anchor_s[:, :, None] + depths[None, :, :] * direct_s[:, :, None]
    pieces = [points]
    for level in range(NFREQ):
        scaled = points * 2.0**level
        pieces.append(jnp.sin(scaled))
        pieces.append(jnp.cos(scaled))
    encoded = jnp.concatenate(pieces, axis=0)
    return encoded.reshape(encoded.shape[0], -1).astype(jnp.bfloat16)


def render_slots(raw_out, step_s, count_s):
    capacity = step_s.shape[0]
    raw_cube = raw_out.reshape(4, capacity, -1)
    samples = raw_cube.shape[2]
    density = jax.nn.softplus(raw_cube[0])
    albedo = jax.nn.sigmoid(raw_cube[1:])
    live_mask = (jnp.arange(samples, dtype=jnp.int32)[None, :] < count_s[:, None]).astype(
        jnp.float32
    )
    optical = density * step_s[:, None] * live_mask
    reached = jnp.cumsum(optical, axis=1)
    sample_weight = jnp.exp(optical - reached) - jnp.exp(-reached)
    colors = jnp.sum(sample_weight[None] * albedo, axis=2)
    log_trans = -reached[:, -1]
    return (colors, log_trans)


def mlp_forward(encoded, weight_in, weight_mid, weight_out):
    hidden_one = jax.nn.relu(
        jnp.dot(weight_in, encoded, preferred_element_type=jnp.float32)
    ).astype(jnp.bfloat16)
    hidden_two = jax.nn.relu(
        jnp.dot(weight_mid, hidden_one, preferred_element_type=jnp.float32)
    ).astype(jnp.bfloat16)
    raw_out = jnp.dot(weight_out, hidden_two, preferred_element_type=jnp.float32)
    return (hidden_one, hidden_two, raw_out)


def outer_sum(left, right):
    return lax.dot_general(
        left, right, (((1,), (1,)), ((), ())), preferred_element_type=jnp.float32
    )


def back_dot(weight, grad):
    return lax.dot_general(
        weight, grad, (((0,), (0,)), ((), ())), preferred_element_type=jnp.float32
    )


def mlp_backward(encoded, hidden_one, hidden_two, d_raw, weight_mid, weight_out):
    d_low = d_raw.astype(jnp.bfloat16)
    grad_o = outer_sum(d_low, hidden_two)
    d_two = (back_dot(weight_out, d_low) * (hidden_two > 0)).astype(jnp.bfloat16)
    grad_m = outer_sum(d_two, hidden_one)
    d_one = (back_dot(weight_mid, d_two) * (hidden_one > 0)).astype(jnp.bfloat16)
    grad_i = outer_sum(d_one, encoded)
    return (grad_i, grad_m, grad_o)


def depth_ranks(order_g, partitions):
    positions = jnp.arange(partitions, dtype=jnp.int32)
    matches = order_g[:, :, None] == positions[None, None, :]
    return jnp.sum(jnp.where(matches, positions[None, :, None], 0), axis=1)


def local(anchor, direct, entry, step, counts, crossing, order, target, w_in, w_mid, w_out):
    highest = lax.Precision.HIGHEST
    partition = lax.axis_index("dom")
    partitions = lax.axis_size("dom")
    capacity = RAYS_DEV * min(4 * K, partitions)
    selector_f, anchor_s, direct_s, entry_s, step_s, count_s = slot_inputs(
        crossing[0], partition, anchor[:, 0], direct[:, 0], entry[0], step[0], counts[0], capacity
    )
    encoded = encode_points(anchor_s, direct_s, entry_s, step_s)
    hidden_one, hidden_two, raw_out = mlp_forward(encoded, w_in[0], w_mid[0], w_out[0])
    outputs, unravel = jax.vjp(lambda values: render_slots(values, step_s, count_s), raw_out)
    color_ray = jnp.dot(
        outputs[0], selector_f, precision=highest, preferred_element_type=jnp.float32
    )
    log_ray = jnp.dot(
        outputs[1][None, :], selector_f, precision=highest, preferred_element_type=jnp.float32
    )[0]
    ray_count = log_ray.shape[0]
    own_rays = ray_count // partitions
    first_ray = partition * own_rays
    depth_rank = depth_ranks(order[0], partitions)
    my_rank = lax.dynamic_slice_in_dim(depth_rank, partition, 1, 1)
    ahead_own = (depth_rank < my_rank).astype(jnp.float32)
    behind_own = (depth_rank > my_rank).astype(jnp.float32)
    log_all = lax.all_gather(log_ray[None], "dom", axis=0, tiled=True)
    before = jnp.einsum(
        "be,ebj->bj", ahead_own, log_all.reshape(partitions, NB, -1), precision=highest
    ).reshape(ray_count)
    total_log = jnp.sum(log_all, axis=0)
    fade_own = jnp.exp(before)
    weighted = fade_own[None, :] * color_ray
    summed = lax.psum_scatter(weighted, "dom", scatter_dimension=1, tiled=True)
    rendered = (
        summed + jnp.exp(lax.dynamic_slice_in_dim(total_log, first_ray, own_rays, 0))[None, :]
    )
    residual_own = rendered - lax.dynamic_slice_in_dim(target[:, 0], first_ray, own_rays, 1)
    residual_all = lax.all_gather(residual_own, "dom", axis=1, tiled=True)
    shares = jnp.sum(residual_all * weighted, axis=0)
    share_all = lax.all_gather(shares[None], "dom", axis=0, tiled=True)
    background = jnp.exp(total_log) * jnp.sum(residual_all, axis=0)
    dlog_ray = (
        jnp.einsum(
            "be,ebj->bj", behind_own, share_all.reshape(partitions, NB, -1), precision=highest
        ).reshape(ray_count)
        + background
    )
    dcolor_ray = fade_own[None, :] * residual_all
    dcolor_s = jnp.dot(
        dcolor_ray, selector_f.T, precision=highest, preferred_element_type=jnp.float32
    )
    dlog_s = jnp.dot(
        dlog_ray[None, :], selector_f.T, precision=highest, preferred_element_type=jnp.float32
    )[0]
    d_raw = unravel((dcolor_s, dlog_s))[0]
    grad_i, grad_m, grad_o = mlp_backward(
        encoded, hidden_one, hidden_two, d_raw, w_mid[0], w_out[0]
    )
    grad_i, grad_m, grad_o = lax.psum((grad_i, grad_m, grad_o), "ray")
    return (rendered[:, None, :], grad_i[None], grad_m[None], grad_o[None])


def solution(mesh):
    in_specs = (
        P(None, "ray", None),
        P(None, "ray", None),
        P("ray", None, None),
        P("ray", None, None),
        P("ray", None, None),
        P("ray", None, None),
        P("ray", None, None),
        P(None, "ray", None),
        P("dom", None, None),
        P("dom", None, None),
        P("dom", None, None),
    )
    out_specs = (
        P(None, "ray", "dom"),
        P("dom", None, None),
        P("dom", None, None),
        P("dom", None, None),
    )
    return jax.shard_map(local, mesh=mesh, in_specs=in_specs, out_specs=out_specs, check_vma=False)
```

profile of v0, /device:TPU:6, one launch (start us, length us, event | category | flops | bytes accessed | tf_op | source)
XLA Modules:
  0.0 727.2 jit_solution(17121550960731183226)
XLA Ops:
  7.3 0.7 select_reduce_fusion.4
  8.0 0.3 reduce-window.9
  8.8 0.8 convolution_bitcast_fusion.4
  9.6 0.9 convolution_bitcast_fusion.5
  10.5 0.8 select_reduce_fusion.2
  11.7 0.2 broadcast_reduce_fusion
  12.5 0.4 cosine_convert_fusion
  13.0 4.7 sine_convert_fusion
  17.7 1.3 concatenate.5
  19.1 0.7 fusion
  19.9 0.7 fusion.1
  20.6 0.6 copy-done.1
  21.2 0.6 convolution_bitcast_fusion
  22.1 0.2 reduce_window_sum.44
  22.6 0.7 fusion.25
  23.4 106.3 %all-gather.2 = f32[128,1,512]{2,1,0:T(1,128)S(1)} all-gather(f32[1,1,512]{2,1,0:T(1,128)S(1)} %convolution_bitcast_fusion.3), channel_id=2, replica_groups=mesh['dom'=128,'ray'=4] {'dom'}, dimensions={0}, use_global_device_ids=true | all-gather | bytes 264192 | tf_op jit(solution)/shard_map/all_gather | solution.py:134
  129.8 0.8 reduce_sum.104
  131.1 0.6 compare_bitcast_fusion
  131.7 1.0 div.8
  132.7 0.3 fusion.57
  133.1 0.8 constant_dynamic-slice_fusion
  133.9 0.8 dynamic-slice_exponential_fusion
  134.7 0.8 convolution_multiply_fusion
  135.6 239.1 %all-reduce.3 = f32[3,512]{1,0:T(4,128)S(1)} all-reduce(f32[3,512]{1,0:T(4,128)S(1)} %convolution_multiply_fusion), channel_id=4, replica_groups=mesh['dom'=128,'ray'=4] {'dom'}, use_global_device_ids=true, to_apply=%region_10.11.clone | all-reduce | flops 1536 | bytes 12288
  374.7 1.3 dynamic-slice.1
  376.6 0.6 fusion.65
  377.3 112.3 %all-gather.3 = f32[128,4,3]{2,1,0:T(4,128)S(1)} all-gather(f32[1,4,3]{2,1,0:T(4,128)S(1)} %bitcast.129), channel_id=1, replica_groups=mesh['dom'=128,'ray'=4] {'dom'}, dimensions={0}, use_global_device_ids=true | all-gather | bytes 6192 | tf_op jit(solution)/shard_map/all_gather | solution.py:146
  489.7 0.6 fusion.63
  490.3 0.8 fusion.14
  491.2 0.3 reduce.7
  491.4 0.7 fusion.22
  492.8 97.8 %all-gather.4 = f32[128,1,512]{2,1,0:T(1,128)S(1)} all-gather(f32[1,1,512]{2,1,0:T(1,128)} %bitcast.128), channel_id=3, replica_groups=mesh['dom'=128,'ray'=4] {'dom'}, dimensions={0}, use_global_device_ids=true | all-gather | bytes 264192 | tf_op jit(solution)/shard_map/all_gather | solution.py:148
  590.7 1.0 fusion.55
  591.8 0.7 multiply_add_fusion.2
  592.5 0.8 fusion.7
  593.4 0.8 add_bitcast_fusion
  594.1 0.4 reduce_window_sum.47
  594.6 0.7 fusion.46
  595.4 1.0 convolution_bitcast_fusion.2
  596.4 2.7 fusion.2
  599.1 4.2 fusion.5
  603.5 3.0 convolution_bitcast_fusion.1
  606.6 0.6 copy.51
  607.1 49.5 %all-reduce.10.cloned.1.call-done = (f32[1,256,63]{1,2,0:T(8,128)}, f32[1,4,256]{2,1,0:T(4,128)}) async-done(((f32[1,256,63]{1,2,0:T(8,128)}, f32[1,4,256]{2,1,0:T(4,128)}), (f32[1,256,63]{1,2,0:T(8,128)}, f32[1,4,256]{2,1,0:T(4,128)})) %all-reduce.10.cloned.1.call-update) | async-done | bytes 68624 | tf_op jit(solution)/shard_map/psum | solution.py:167
  656.6 1.5 copy.52
  658.1 59.4 %all-reduce.8.cloned.1.call-done = f32[1,256,256]{2,1,0:T(8,128)} async-done(((f32[1,256,256]{2,1,0:T(8,128)}), f32[1,256,256]{2,1,0:T(8,128)}) %all-reduce.8.cloned.1.call-update) | async-done | bytes 262160 | tf_op jit(solution)/shard_map/psum | solution.py:167
  717.5 1.7 copy.78
  719.1 1.3 copy.79
  (72 shorter events, 4.2 us)
Async XLA Ops:
  7.2 12.7 %copy-start = (bf16[1,256,256]{2,1,0:T(8,128)(2,1)S(1)}, bf16[1,256,256]{2,1,0:T(8,128)(2,1)}, u32[]{:S(2)}) copy-start(bf16[1,256,256]{2,1,0:T(8,128)(2,1)} %param.20) | copy-start | bytes 393220
  7.2 11.9 %copy-start.4 = (bf16[1,256,63]{1,2,0:T(8,128)(2,1)S(1)}, bf16[1,256,63]{1,2,0:T(8,128)(2,1)}, u32[]{:S(2)}) copy-start(bf16[1,256,63]{1,2,0:T(8,128)(2,1)} %param.19) | copy-start | bytes 96772
  7.2 649.4 %all-reduce.10.cloned.1.call-start = ((), (), s32[]{:S(2)}) async-start(), calls=%async_computation.1 | async-start | bytes 139264 | tf_op jit(solution)/shard_map/psum | solution.py:167
  8.0 15.3 %copy-start.9 = (pred[512]{0:T(512)(128)(4,1)}, pred[512]{0:T(512)(128)(4,1)S(1)}, u32[]{:S(2)}) copy-start(pred[512]{0:T(512)(128)(4,1)S(1)} %reduce_or.9) | copy-start | bytes 1540
  8.7 14.6 %copy-start.8 = (s32[512]{0:T(512)}, s32[512]{0:T(512)S(1)}, u32[]{:S(2)}) copy-start(s32[512]{0:T(512)S(1)} %add_bitcast_fusion.1) | copy-start | bytes 6148
  8.8 13.7 %copy-start.6 = (s32[64]{0:T(128)}, s32[64]{0:T(128)S(1)}, u32[]{:S(2)}) copy-start(s32[64]{0:T(128)S(1)} %select_reduce_fusion.1) | copy-start | bytes 772
  11.4 11.1 %copy-start.5 = (f32[64]{0:T(128)}, f32[64]{0:T(128)S(1)}, u32[]{:S(2)}) copy-start(f32[64]{0:T(128)S(1)} %convolution_bitcast_fusion.7) | copy-start | bytes 772
  19.8 1.4 copy-start.1
  19.9 1.3 copy-start.11
  21.2 109.5 %copy-start.10 = (s32[1,8,128]{2,1,0:T(8,128)S(1)}, s32[1,8,128]{2,1,0:T(8,128)}, u32[]{:S(2)}) copy-start(s32[1,8,128]{2,1,0:T(8,128)} %param.17) | copy-start | bytes 12292
  492.2 103.1 %copy-start.3 = (f32[3,64,64]{2,1,0:T(8,128)S(1)}, f32[3,64,64]{2,1,0:T(8,128)}, u32[]{:S(2)}) copy-start(f32[3,64,64]{2,1,0:T(8,128)} %fusion.22) | copy-start | bytes 147460
  599.1 4.3 copy-start.2
  603.4 3.1 copy-start.7
  603.4 114.0 %all-reduce.8.cloned.1.call-start = ((), (), s32[]{:S(2)}) async-start(), calls=%async_computation | async-start | bytes 524288 | tf_op jit(solution)/shard_map/psum | solution.py:167
Sparse Core Ops, SparseCore 0:
  603.5 53.0 all-reduce.9
  659.6 57.8 all-reduce.7
where the time goes:
time: 728 us; the launch traced here: 727 us
  blocking collectives  555 us (76%)
  waiting for transfers between devices  109 us (15%)
  matrix products  19.1 us (3%)
  other arithmetic  15.2 us (2%)
  between operations  15.1 us (2%)
  local copies, waits for them, and re-layouts  13.5 us (2%)
    unnamed x1, blocking collectives  239 us
    all_gather x1, blocking collectives, local(): residual_all = lax.all_gather(residual_own, 'dom', axis=1, tiled=True)  112 us
    psum x2, waiting for transfers between devices, local(): grad_i, grad_m, grad_o = lax.psum((grad_i, grad_m, grad_o), 'ray')  109 us
    all_gather x1, blocking collectives, local(): log_all = lax.all_gather(log_ray[None], 'dom', axis=0, tiled=True)  106 us
    all_gather x1, blocking collectives, local(): share_all = lax.all_gather(shares[None], 'dom', axis=0, tiled=True)  97.8 us
  transfers between devices with their start and end apart: 2, of which 2 were waited for; matrix products, arithmetic and copies ran while one was open for 1% of the time, Pallas kernels for 0%

commit v1 on v0

v1 whole, which is shorter than its diff:
```python
import functools

import jax
import jax.numpy as jnp
from jax import lax
from jax.experimental import pallas as pl
from jax.experimental.pallas import tpu as pltpu
from jax.sharding import PartitionSpec as P

NFREQ = 10
FEATS = 63
S = 64
K = 4
NB = 8
CAP = 64
ZONES = 128
RG = 512
OWN = 4
ROWS = 32
SEL = 72
COLS = CAP * S
TILE = 4
CHUNK = 88
F32 = jnp.float32
BF16 = jnp.bfloat16


def iota(shape, dim):
    return lax.broadcasted_iota(jnp.int32, shape, dim)


def split3(x):
    high = x.astype(BF16)
    rest = x - high.astype(F32)
    mid = rest.astype(BF16)
    low = (rest - mid.astype(F32)).astype(BF16)
    return high, mid, low


def dot(a, b):
    return jnp.dot(a, b, preferred_element_type=F32)


def dot_nt(a, b):
    return lax.dot_general(a, b, (((1,), (1,)), ((), ())), preferred_element_type=F32)


def split_dot(x, exact):
    return sum(dot(part, exact) for part in split3(x))


def halves(column):
    lane = iota((ROWS, 2 * S), 1)
    return jnp.where(lane < S, column[0:ROWS], column[ROWS : 2 * ROWS])


def sin_cos(x):
    turns = jnp.floor(x * 0.6366197723675814 + 0.5)
    r = ((x - turns * 1.5703125) - turns * 4.837512969970703e-4) - turns * 7.54978995489188e-8
    z = r * r
    s = ((-1.9515295891e-4 * z + 8.3321608736e-3) * z - 1.6666654611e-1) * z * r + r
    c = ((2.443315711809948e-5 * z - 1.388731625493765e-3) * z + 4.166664568298827e-2) * z * z - 0.5 * z + 1.0
    quadrant = turns.astype(jnp.int32)
    swap = (quadrant & 1) == 1
    sin_r = jnp.where(swap, c, s)
    cos_r = jnp.where(swap, s, c)
    sin_r = jnp.where((quadrant & 2) == 2, -sin_r, sin_r)
    cos_r = jnp.where(((quadrant + 1) & 2) == 2, -cos_r, cos_r)
    return sin_r, cos_r


def shade(raw, step_d, count_d):
    lane = iota((ROWS, 2 * S), 1)
    index = lane & (S - 1)
    scale = jnp.where(index.astype(F32) < count_d, step_d, 0.0)
    decay = jnp.exp(-jnp.abs(raw[0]))
    density = jnp.maximum(raw[0], 0.0) + jnp.log1p(decay)
    optical = density * scale
    source, target = iota((2 * S, 2 * S), 0), iota((2 * S, 2 * S), 1)
    upto = ((source <= target) & ((source < S) == (target < S))).astype(F32).astype(BF16)
    reached = split_dot(optical, upto)
    entering = jnp.exp(optical - reached)
    weight = entering - jnp.exp(-reached)
    albedo = [1.0 / (1.0 + jnp.exp(-raw[c])) for c in (1, 2, 3)]
    return scale, optical, entering, weight, albedo


def forward_kernel(
    part_ref, anchor_ref, direct_ref, entry_ref, step_ref, counts_ref, crossing_ref, target_ref,
    w_in_ref, w_mid_ref, w_out_ref,
    send_ref, enc_ref, one_ref, two_ref, raw_ref, reals_ref, whole_ref,
    vals, ints, ranks, feats, win,
):
    part = part_ref[0]
    zone = iota((ZONES, RG), 0)
    crossing = crossing_ref[0]
    names = [zone == crossing[k : k + 1] for k in range(K)]
    member = names[0] | names[1] | names[2] | names[3]
    earlier = (iota((RG, RG), 0) < iota((RG, RG), 1)).astype(F32).astype(BF16)
    ranks[...] = dot(member.astype(F32).astype(BF16), earlier)
    place_all = ranks[...]
    own = crossing == part
    crossed = own[0:1] | own[1:2] | own[2:3] | own[3:4]

    def of_own(ref):
        return jnp.sum(jnp.where(own, ref[0].astype(F32), 0.0), axis=0, keepdims=True)

    vals[...] = jnp.zeros_like(vals)
    for d in range(3):
        vals[d : d + 1] = anchor_ref[d]
        vals[3 + d : 4 + d] = direct_ref[d]
        vals[8 + d : 9 + d] = target_ref[d]
    vals[6:7] = of_own(entry_ref)
    vals[7:8] = of_own(step_ref)
    ints[...] = jnp.zeros_like(ints)
    ints[0:4] = crossing.astype(F32)
    for k in range(K):
        ints[4 + k : 5 + k] = jnp.sum(jnp.where(names[k], place_all, 0.0), axis=0, keepdims=True)
    ray = iota((1, RG), 1)
    ints[8:9] = of_own(counts_ref)
    ints[9:10] = (ray // (RG // NB)).astype(F32)
    ints[10:11] = jnp.ones((1, RG), F32)

    row = iota((SEL, RG), 0)
    place_own = ranks[pl.ds(part, 1), :].astype(jnp.int32)
    place_own = jnp.where(crossed, place_own, -1)
    in_slot = (row < CAP) & (place_own == row)
    own_ray = (row >= CAP) & (row < CAP + OWN) & (ray == part * OWN + (row - CAP))
    selector = (in_slot | own_ray).astype(F32).astype(BF16)
    reals = sum(dot_nt(selector, piece) for piece in split3(vals[...]))
    whole = dot_nt(selector, ints[...].astype(BF16))
    reals_ref[...] = reals
    whole_ref[...] = whole

    columns = [halves(reals[0:CAP, j : j + 1]) for j in range(8)]
    count_d = halves(whole[0:CAP, 8:9])
    step_d = columns[7]
    index = (iota((ROWS, 2 * S), 1) & (S - 1)).astype(F32)
    depth = columns[6] + (index + 0.5) * step_d
    feats[FEATS * ROWS : (FEATS + 1) * ROWS] = jnp.zeros((ROWS, 2 * S), F32)
    for d in range(3):
        point = columns[d] + depth * columns[3 + d]
        feats[d * ROWS : (d + 1) * ROWS] = point
        sin_x, cos_x = sin_cos(point)
        for level in range(NFREQ):
            at = 3 + 6 * level + d
            feats[at * ROWS : (at + 1) * ROWS] = sin_x
            feats[(at + 3) * ROWS : (at + 4) * ROWS] = cos_x
            sin_x, cos_x = 2.0 * sin_x * cos_x, 1.0 - 2.0 * sin_x * sin_x

    win[...] = jnp.zeros_like(win)
    win[0:FEATS] = w_in_ref[...].astype(F32)
    w_in = win[...].T.astype(BF16)
    w_mid = w_mid_ref[...]
    w_out = w_out_ref[...]
    for tile in range(ROWS // TILE):
        span = slice(tile * TILE * 128, (tile + 1) * TILE * 128)
        encoded = jnp.concatenate(
            [feats[pl.ds(tile * TILE + j, FEATS + 1, stride=ROWS), :].astype(BF16) for j in range(TILE)], axis=1
        )
        enc_ref[:, span] = encoded
        one = jnp.maximum(dot(w_in, encoded), 0.0).astype(BF16)
        one_ref[:, span] = one
        two = jnp.maximum(dot(w_mid, one), 0.0).astype(BF16)
        two_ref[:, span] = two
        raw = dot(w_out, two)
        for j in range(TILE):
            raw_ref[pl.ds(tile * TILE + j, 4, stride=ROWS), :] = raw[:, j * 128 : (j + 1) * 128]

    raw = [raw_ref[c * ROWS : (c + 1) * ROWS] for c in range(4)]
    _, optical, _, weight, albedo = shade(raw, step_d, count_d)
    sums = jnp.concatenate([weight * albedo[0], weight * albedo[1], weight * albedo[2], -optical], axis=0)
    half = (iota((8, 2 * S), 0) == iota((8, 2 * S), 1) // S).astype(F32).astype(BF16)
    sent = sum(dot_nt(half, piece) for piece in split3(sums))
    send_ref[...] = jnp.broadcast_to(sent[None, 0:2], send_ref.shape)


def backward_kernel(
    part_ref, got_ref, order_ref, reals_ref, whole_ref, raw_ref, enc_ref, one_ref, two_ref, w_mid_ref, w_out_ref,
    rendered_ref, grads_ref,
    draw, wout,
):
    part = part_ref[0]
    reals, whole = reals_ref[...], whole_ref[...]
    bundle = (whole[:, 9:10].astype(jnp.int32) == iota((SEL, NB), 1)).astype(F32).astype(BF16)
    order = dot(bundle, order_ref[0].astype(F32).astype(BF16))
    lane = iota((SEL, ZONES), 1)
    position = lane.astype(F32)
    named = [whole[:, k : k + 1] for k in range(K)]
    rank = [jnp.sum(jnp.where(order == named[k], position, 0.0), axis=1, keepdims=True) for k in range(K)]
    pick = jnp.concatenate([(named[k] == position).astype(F32).astype(BF16) for k in range(K)], axis=0)
    place = jnp.concatenate([whole[:, 4 + k : 5 + k] for k in range(K)], axis=0).astype(jnp.int32)
    pieces = [split3(got_ref[:, h, :]) for h in range(2)]
    wanted = (iota((K * SEL, ZONES), 1) % ROWS) == (place % ROWS)
    gather = (iota((ZONES, 8), 0) // ROWS == iota((ZONES, 8), 1)).astype(F32).astype(BF16)
    values = jnp.zeros((K * SEL, 8), F32)
    for piece in range(3):
        low, high = dot(pick, pieces[0][piece]), dot(pick, pieces[1][piece])
        found = jnp.where(wanted, jnp.where(place < ROWS, low, high), 0.0)
        values = values + dot(found.astype(BF16), gather)

    mine = [values[k * SEL : (k + 1) * SEL] for k in range(K)]
    log = [mine[k][:, 3:4] for k in range(K)]
    color = [[mine[k][:, c : c + 1] for c in range(3)] for k in range(K)]
    ahead = [[rank[j] < rank[k] for j in range(K)] for k in range(K)]
    fade = [jnp.exp(sum(jnp.where(ahead[k][j], log[j], 0.0) for j in range(K) if j != k)) for k in range(K)]
    clear = jnp.exp(log[0] + log[1] + log[2] + log[3])
    rendered = [sum(fade[k] * color[k][c] for k in range(K)) + clear for c in range(3)]
    residual = [rendered[c] - reals[:, 8 + c : 9 + c] for c in range(3)]
    share = [fade[k] * sum(residual[c] * color[k][c] for c in range(3)) for k in range(K)]
    owned = [named[k] == part.astype(F32) for k in range(K)]
    own_rank = sum(jnp.where(owned[k], rank[k], 0.0) for k in range(K))
    own_fade = sum(jnp.where(owned[k], fade[k], 0.0) for k in range(K))
    dlog = sum(jnp.where(rank[k] > own_rank, share[k], 0.0) for k in range(K))
    dlog = dlog + clear * (residual[0] + residual[1] + residual[2])
    used = whole[:, 10:11] > 0.5
    dlog = jnp.where(used, dlog, 0.0)
    dcolor = [jnp.where(used, own_fade * residual[c], 0.0) for c in range(3)]
    diagonal = iota((8, 8), 0) == iota((8, 8), 1)
    for c in range(3):
        line = jnp.sum(jnp.where(diagonal, rendered[c][CAP:SEL], 0.0), axis=0, keepdims=True)
        rendered_ref[c] = line[:, 0:OWN]

    raw = [raw_ref[c * ROWS : (c + 1) * ROWS] for c in range(4)]
    step_d = halves(reals[0:CAP, 7:8])
    count_d = halves(whole[0:CAP, 8:9])
    scale, _, entering, weight, albedo = shade(raw, step_d, count_d)
    dcolor_d = [halves(dcolor[c][0:CAP]) for c in range(3)]
    gain = sum(dcolor_d[c] * albedo[c] for c in range(3))
    source, target = iota((2 * S, 2 * S), 0), iota((2 * S, 2 * S), 1)
    since = ((source >= target) & ((source < S) == (target < S))).astype(F32).astype(BF16)
    behind = split_dot(gain * weight, since)
    d_optical = gain * entering - behind - halves(dlog[0:CAP])
    draw[0:ROWS] = d_optical * scale / (1.0 + jnp.exp(-raw[0]))
    for c in range(3):
        draw[(c + 1) * ROWS : (c + 2) * ROWS] = weight * dcolor_d[c] * albedo[c] * (1.0 - albedo[c])
    draw[4 * ROWS :] = jnp.zeros((12 * ROWS, 2 * S), F32)

    wout[...] = jnp.zeros_like(wout)
    wout[0:4] = w_out_ref[...].astype(F32)
    w_out_t = wout[...].T.astype(BF16)
    w_mid_t = w_mid_ref[...].astype(F32).T.astype(BF16)
    grad_out = jnp.zeros((16, 256), F32)
    grad_mid = jnp.zeros((256, 256), F32)
    grad_in = jnp.zeros((64, 256), F32)
    for tile in range(ROWS // TILE):
        span = slice(tile * TILE * 128, (tile + 1) * TILE * 128)
        low = jnp.concatenate(
            [draw[pl.ds(tile * TILE + j, 16, stride=ROWS), :].astype(BF16) for j in range(TILE)], axis=1
        )
        two, one = two_ref[:, span], one_ref[:, span]
        grad_out = grad_out + dot_nt(low, two)
        d_two = jnp.where(two > 0, dot(w_out_t, low), 0.0).astype(BF16)
        grad_mid = grad_mid + dot_nt(d_two, one)
        d_one = jnp.where(one > 0, dot(w_mid_t, d_two), 0.0).astype(BF16)
        grad_in = grad_in + dot_nt(enc_ref[:, span], d_one)
    for q in range(4):
        grads_ref[q, 0:64] = grad_mid[64 * q : 64 * q + 64]
        grads_ref[q, 64:80] = grad_in[16 * q : 16 * q + 16]
        grads_ref[q, 80:88] = jnp.broadcast_to(grad_out[q : q + 1], (8, 256))


def unpack_kernel(all_ref, in_ref, mid_ref, out_ref):
    for q in range(4):
        mid_ref[64 * q : 64 * q + 64] = all_ref[q, 0:64]
        rows = min(16, FEATS - 16 * q)
        in_ref[16 * q : 16 * q + rows, 0, :] = all_ref[q, 64 : 64 + rows]
        out_ref[q : q + 1] = all_ref[q, 80:81]


def vmem(count):
    return [pl.BlockSpec(memory_space=pltpu.VMEM)] * count


def local(anchor, direct, entry, step, counts, crossing, order, target, w_in, w_mid, w_out):
    part = lax.axis_index("dom").astype(jnp.int32).reshape(1)
    entry, step, counts, crossing = (jnp.swapaxes(a, 1, 2) for a in (entry, step, counts, crossing))
    w_in_t = jnp.swapaxes(w_in, 1, 2)[0]
    scalar = pl.BlockSpec(memory_space=pltpu.SMEM)
    params = pltpu.CompilerParams(vmem_limit_bytes=40 * 1024 * 1024)
    shape = jax.ShapeDtypeStruct
    send, enc, one, two, raw, reals, whole = pl.pallas_call(
        forward_kernel,
        out_shape=(
            shape((ZONES, 2, 128), F32),
            shape((64, COLS), BF16),
            shape((256, COLS), BF16),
            shape((256, COLS), BF16),
            shape((4 * ROWS, 128), F32),
            shape((SEL, 16), F32),
            shape((SEL, 16), F32),
        ),
        in_specs=[scalar] + vmem(10),
        out_specs=vmem(7),
        scratch_shapes=[
            pltpu.VMEM((16, RG), F32),
            pltpu.VMEM((16, RG), F32),
            pltpu.VMEM((ZONES, RG), F32),
            pltpu.VMEM((64 * ROWS, 128), F32),
            pltpu.VMEM((64, 256), F32),
        ],
        compiler_params=params,
        name="forward",
    )(part, anchor, direct, entry, step, counts, crossing, target, w_in_t, w_mid[0], w_out[0])
    got = lax.all_to_all(send, "dom", 0, 0)
    rendered, grads = pl.pallas_call(
        backward_kernel,
        out_shape=(shape((3, 1, OWN), F32), shape((4, CHUNK, 256), F32)),
        in_specs=[scalar] + vmem(10),
        out_specs=vmem(2),
        scratch_shapes=[pltpu.VMEM((16 * ROWS, 128), F32), pltpu.VMEM((16, 256), F32)],
        compiler_params=params,
        name="backward",
    )(part, got, order, reals, whole, raw, enc, one, two, w_mid[0], w_out[0])
    shares = lax.all_to_all(grads, "ray", 0, 0)
    total = jnp.sum(shares, axis=0)
    everything = lax.all_to_all(jnp.broadcast_to(total[None], grads.shape), "ray", 0, 0)
    grad_i, grad_m, grad_o = pl.pallas_call(
        unpack_kernel,
        out_shape=(shape((FEATS, 1, 256), F32), shape((256, 256), F32), shape((4, 256), F32)),
        in_specs=vmem(1),
        out_specs=vmem(3),
        compiler_params=params,
        name="unpack",
    )(everything)
    return rendered, jnp.transpose(grad_i, (1, 2, 0)), grad_m[None], grad_o[None]


def solution(mesh):
    in_specs = (
        P(None, "ray", None),
        P(None, "ray", None),
        P("ray", None, None),
        P("ray", None, None),
        P("ray", None, None),
        P("ray", None, None),
        P("ray", None, None),
        P(None, "ray", None),
        P("dom", None, None),
        P("dom", None, None),
        P("dom", None, None),
    )
    out_specs = (
        P(None, "ray", "dom"),
        P("dom", None, None),
        P("dom", None, None),
        P("dom", None, None),
    )
    return jax.shard_map(local, mesh=mesh, in_specs=in_specs, out_specs=out_specs, check_vma=False)
```

time: 728 us -> 78.5 us (0.11)
  blocking collectives: 555 us -> 57.2 us
  waiting for transfers between devices: 109 us -> 0 us
  matrix products: 19.1 us -> 0 us
  other arithmetic: 15.2 us -> 0.02 us
  between operations: 15.1 us -> 0.69 us
  Pallas kernels: 0 us -> 10.5 us
    all_gather x3 -> x0, blocking collectives: 316 us -> none  [the longest x1 112 us: local(): residual_all = lax.all_gather(residual_own, 'dom', axis=1, tiled=True)]
    unnamed x1 -> x0, blocking collectives: 239 us -> none
    psum x2 -> x0, waiting for transfers between devices: 109 us -> none  [local(): grad_i, grad_m, grad_o = lax.psum((grad_i, grad_m, grad_o), 'ray')]
    all_to_all x0 -> x3, blocking collectives: none -> 57.2 us  [the longest x1 35.3 us: local(): got = lax.all_to_all(send, 'dom', 0, 0)]
    dot_general x17 -> x0, matrix products: 19.1 us -> none  [the longest x3 8.26 us: outer_sum(): lax.dot_general(left, right, (((1,), (1,)), ((), ())), preferred_element_...]
    pallas_call x0 -> x3, Pallas kernels: none -> 10.5 us  [the longest x1 5.2 us: local(): pl.pallas_call(backward_kernel, out_shape=(shape((3, 1, OWN), F32), shape...]
  transfers between devices with their start and end apart: 2 -> 0, of which waited for: 2 -> 0; matrix products, arithmetic and copies ran while one was open for 1% -> 0% of each run, Pallas kernels for 0% -> 0%
where the time goes in v1:
time: 78.5 us; the launch traced here: 77.2 us
  blocking collectives  57.2 us (73%)
  Pallas kernels  10.5 us (13%)
  local copies, waits for them, and re-layouts  8.81 us (11%)
    all_to_all x1, blocking collectives, local(): got = lax.all_to_all(send, 'dom', 0, 0)  35.3 us
    all_to_all x1, blocking collectives, local(): shares = lax.all_to_all(grads, 'ray', 0, 0)  12.4 us
    all_to_all x1, blocking collectives, local(): lax.all_to_all(jnp.broadcast_to(total[None], grads.shape), 'ray', 0, 0)  9.59 us
    unnamed x24, local copies, waits for them, and re-layouts  8.79 us
    pallas_call x1, Pallas kernels, local(): pl.pallas_call(backward_kernel, out_shape=(shape((3, 1, OWN), F32), shape...  5.2 us
    pallas_call x1, Pallas kernels, local(): pl.pallas_call(forward_kernel, out_shape=(shape((ZONES, 2, 128), F32), sh...  4.51 us

profile of v1, /device:TPU:6, one launch (start us, length us, event | category | flops | bytes accessed | tf_op | source)
XLA Modules:
  0.0 77.2 jit_solution(3520035463995608222)
XLA Ops:
  0.6 0.0 copy-start
  0.7 0.9 %copy-done = bf16[1,256,256]{2,1,0:T(8,128)(2,1)S(1)} copy-done((bf16[1,256,256]{2,1,0:T(8,128)(2,1)S(1)}, bf16[1,256,256]{2,1,0:T(8,128)(2,1)}, u32[]{:S(2)}) %copy-start) | copy-done | bytes 131096
  1.5 0.0 copy-start.2
  1.5 0.8 copy-done.2
  2.3 0.0 copy-start.3
  2.3 0.7 copy-done.3
  3.0 0.0 copy-start.4
  3.0 0.7 copy-done.4
  3.7 0.0 copy-start.5
  3.7 0.7 copy-done.5
  4.4 0.0 copy-start.6
  4.4 0.7 copy-done.6
  5.1 0.0 copy-start.7
  5.1 0.7 copy-done.7
  5.8 0.0 copy-start.8
  5.8 0.7 copy-done.8
  6.5 0.0 copy-start.9
  6.5 0.7 copy-done.9
  7.2 0.0 copy-start.10
  7.2 0.7 copy-done.10
  7.9 4.5 %forward.1 = (f32[128,2,128]{2,1,0:T(2,128)S(1)}, bf16[64,4096]{1,0:T(8,128)(2,1)S(1)}, bf16[256,4096]{1,0:T(8,128)(2,1)S(1)}, bf16[256,4096]{1,0:T(8,128)(2,1)S...) custom-call(s32[1]{0:T(128)} %bitcast.part_ref, f32[3,1,512]{2,1,0:T(1,128)S(1)} %copy-done.8, ...), custom_call_target="tpu_custom_call" | custom-call | tf_op jit(solution)/shard_map/forward/pallas_call | solution.py:282
  12.4 35.3 %all_to_all.15.got_ref = f32[128,2,128]{2,1,0:T(2,128)S(1)} all-to-all(f32[128,2,128]{2,1,0:T(2,128)S(1)} %get-tuple-element.16), channel_id=1, replica_groups=mesh['dom'=128,'ray'=4] {'dom'}, dimensions={0} | all-to-all | bytes 262144 | tf_op jit(solution)/shard_map/all_to_all | solution.py:305
  47.7 0.0 copy-start.1
  47.7 0.9 %copy-done.1 = bf16[1,256,256]{2,1,0:T(8,128)(2,1)S(1)} copy-done((bf16[1,256,256]{2,1,0:T(8,128)(2,1)S(1)}, bf16[1,256,256]{2,1,0:T(8,128)(2,1)}, u32[]{:S(2)}) %copy-start.1) | copy-done | bytes 131096
  48.6 0.0 copy-start.11
  48.6 0.7 copy-done.11
  49.2 5.2 %backward.1 = (f32[3,1,4]{2,1,0:T(1,128)}, f32[4,88,256]{2,1,0:T(8,128)S(1)}) custom-call(s32[1]{0:T(128)} %bitcast.part_ref, f32[128,2,128]{2,1,0:T(2,128)S(1)} %all_to_all.15.got_ref, s32[1,8,128]{2,1,0:T(8,128)S(1)} %copy-done.11, f32[72,16]{1,0:T(8,128)S(1)} %get-tuple-element.17.reals_ref, f32[72,16]{1,0:T(8,128)S(1)} %get-tuple-element.18.whole_ref, ...), custom_call_target="tpu_custom_call" | custom-call | tf_op jit(solution)/shard_map/backward/pallas_call | solution.py:306
  54.5 12.4 %all_to_all.16 = f32[4,88,256]{2,1,0:T(8,128)S(1)} all-to-all(f32[4,88,256]{2,1,0:T(8,128)S(1)} %get-tuple-element.24), channel_id=1, replica_groups=mesh['dom'=128,'ray'=4] {'ray'}, dimensions={0} | all-to-all | bytes 720896 | tf_op jit(solution)/shard_map/all_to_all | solution.py:315
  66.9 9.6 %all_to_all.17.all_ref = f32[4,88,256]{2,1,0:T(8,128)S(1)} all-to-all(f32[4,88,256]{2,1,0:T(8,128)S(1)} %broadcast_in_dim.12), channel_id=1, replica_groups=mesh['dom'=128,'ray'=4] {'ray'}, dimensions={0} | all-to-all | bytes 720896 | tf_op jit(solution)/shard_map/all_to_all | solution.py:317
  76.5 0.7 unpack.1
  (2 shorter events, 0.0 us)
Async XLA Ops:
  0.6 0.9 %copy-start = (bf16[1,256,256]{2,1,0:T(8,128)(2,1)S(1)}, bf16[1,256,256]{2,1,0:T(8,128)(2,1)}, u32[]{:S(2)}) copy-start(bf16[1,256,256]{2,1,0:T(8,128)(2,1)} %param.20) | copy-start | bytes 393220
  1.5 0.8 copy-start.2
  2.3 0.7 copy-start.3
  3.0 0.7 copy-start.4
  3.7 0.7 copy-start.5
  4.4 0.7 copy-start.6
  5.1 0.7 copy-start.7
  5.8 0.7 copy-start.8
  6.5 0.7 copy-start.9
  7.2 0.7 copy-start.10
  47.7 0.9 %copy-start.1 = (bf16[1,256,256]{2,1,0:T(8,128)(2,1)S(1)}, bf16[1,256,256]{2,1,0:T(8,128)(2,1)}, u32[]{:S(2)}) copy-start(bf16[1,256,256]{2,1,0:T(8,128)(2,1)} %param.20) | copy-start | bytes 393220
  48.6 0.7 copy-start.11

commit v2 on v1

--- a/solution.py
+++ b/solution.py
@@ -86,12 +86,24 @@
 
 
 def forward_kernel(
-    part_ref, anchor_ref, direct_ref, entry_ref, step_ref, counts_ref, crossing_ref, target_ref,
-    w_in_ref, w_mid_ref, w_out_ref,
-    send_ref, enc_ref, one_ref, two_ref, raw_ref, reals_ref, whole_ref,
-    vals, ints, ranks, feats, win,
+    part_ref, anchor_hbm, direct_hbm, entry_hbm, step_hbm, counts_hbm, crossing_hbm, target_hbm, order_hbm,
+    w_in_hbm, w_mid_hbm, w_out_hbm,
+    send_ref, enc_ref, one_ref, two_ref, raw_ref, reals_ref, whole_ref, order_ref, w_mid_ref, w_out_ref,
+    anchor_ref, direct_ref, entry_ref, step_ref, counts_ref, crossing_ref, target_ref, w_in_ref,
+    vals, ints, ranks, feats, win, sems,
 ):
+    copies = [
+        pltpu.make_async_copy(source, target, sems.at[i])
+        for i, (source, target) in enumerate((
+            (crossing_hbm, crossing_ref), (entry_hbm, entry_ref), (step_hbm, step_ref), (counts_hbm, counts_ref),
+            (anchor_hbm, anchor_ref), (direct_hbm, direct_ref), (target_hbm, target_ref), (w_in_hbm, w_in_ref),
+            (w_mid_hbm, w_mid_ref), (w_out_hbm, w_out_ref), (order_hbm, order_ref),
+        ))
+    ]
+    for copy in copies:
+        copy.start()
     part = part_ref[0]
+    copies[0].wait()
     zone = iota((ZONES, RG), 0)
     crossing = crossing_ref[0]
     names = [zone == crossing[k : k + 1] for k in range(K)]
@@ -105,6 +117,8 @@
     def of_own(ref):
         return jnp.sum(jnp.where(own, ref[0].astype(F32), 0.0), axis=0, keepdims=True)
 
+    for copy in copies[1:7]:
+        copy.wait()
     vals[...] = jnp.zeros_like(vals)
     for d in range(3):
         vals[d : d + 1] = anchor_ref[d]
@@ -148,6 +162,8 @@
             feats[(at + 3) * ROWS : (at + 4) * ROWS] = cos_x
             sin_x, cos_x = 2.0 * sin_x * cos_x, 1.0 - 2.0 * sin_x * sin_x
 
+    for copy in copies[7:]:
+        copy.wait()
     win[...] = jnp.zeros_like(win)
     win[0:FEATS] = w_in_ref[...].astype(F32)
     w_in = win[...].T.astype(BF16)
@@ -272,6 +288,10 @@
     return [pl.BlockSpec(memory_space=pltpu.VMEM)] * count
 
 
+def in_hbm(array):
+    return pltpu.with_memory_space_constraint(array, pltpu.HBM)
+
+
 def local(anchor, direct, entry, step, counts, crossing, order, target, w_in, w_mid, w_out):
     part = lax.axis_index("dom").astype(jnp.int32).reshape(1)
     entry, step, counts, crossing = (jnp.swapaxes(a, 1, 2) for a in (entry, step, counts, crossing))
@@ -279,7 +299,7 @@
     scalar = pl.BlockSpec(memory_space=pltpu.SMEM)
     params = pltpu.CompilerParams(vmem_limit_bytes=40 * 1024 * 1024)
     shape = jax.ShapeDtypeStruct
-    send, enc, one, two, raw, reals, whole = pl.pallas_call(
+    send, enc, one, two, raw, reals, whole, order_v, w_mid_v, w_out_v = pl.pallas_call(
         forward_kernel,
         out_shape=(
             shape((ZONES, 2, 128), F32),
@@ -289,19 +309,33 @@
             shape((4 * ROWS, 128), F32),
             shape((SEL, 16), F32),
             shape((SEL, 16), F32),
+            shape((1, NB, ZONES), jnp.int32),
+            shape((256, 256), BF16),
+            shape((4, 256), BF16),
         ),
-        in_specs=[scalar] + vmem(10),
-        out_specs=vmem(7),
+        in_specs=[scalar] + [pl.BlockSpec(memory_space=pltpu.HBM)] * 11,
+        out_specs=vmem(10),
         scratch_shapes=[
+            pltpu.VMEM((3, 1, RG), F32),
+            pltpu.VMEM((3, 1, RG), F32),
+            pltpu.VMEM((1, K, RG), F32),
+            pltpu.VMEM((1, K, RG), F32),
+            pltpu.VMEM((1, K, RG), jnp.int32),
+            pltpu.VMEM((1, K, RG), jnp.int32),
+            pltpu.VMEM((3, 1, RG), F32),
+            pltpu.VMEM((FEATS, 256), BF16),
             pltpu.VMEM((16, RG), F32),
             pltpu.VMEM((16, RG), F32),
             pltpu.VMEM((ZONES, RG), F32),
             pltpu.VMEM((64 * ROWS, 128), F32),
             pltpu.VMEM((64, 256), F32),
+            pltpu.SemaphoreType.DMA((11,)),
         ],
         compiler_params=params,
         name="forward",
-    )(part, anchor, direct, entry, step, counts, crossing, target, w_in_t, w_mid[0], w_out[0])
+    )(part, *(in_hbm(a) for a in (
+        anchor, direct, entry, step, counts, crossing, target, order, w_in_t, w_mid[0], w_out[0]
+    )))
     got = lax.all_to_all(send, "dom", 0, 0)
     rendered, grads = pl.pallas_call(
         backward_kernel,
@@ -311,7 +345,7 @@
         scratch_shapes=[pltpu.VMEM((16 * ROWS, 128), F32), pltpu.VMEM((16, 256), F32)],
         compiler_params=params,
         name="backward",
-    )(part, got, order, reals, whole, raw, enc, one, two, w_mid[0], w_out[0])
+    )(part, got, order_v, reals, whole, raw, enc, one, two, w_mid_v, w_out_v)
     shares = lax.all_to_all(grads, "ray", 0, 0)
     total = jnp.sum(shares, axis=0)
     everything = lax.all_to_all(jnp.broadcast_to(total[None], grads.shape), "ray", 0, 0)

time: 78.5 us -> 70.2 us (0.89)
  local copies, waits for them, and re-layouts: 8.81 us -> 0.03 us
  Pallas kernels: 10.5 us -> 11.4 us
    unnamed x24 -> x0, local copies, waits for them, and re-layouts: 8.79 us -> none
    pallas_call x1, Pallas kernels: 4.51 us -> 5.41 us  [local(): pl.pallas_call(forward_kernel, out_shape=(shape((ZONES, 2, 128), F32), sh...]
where the time goes in v2:
time: 70.2 us; the launch traced here: 69.4 us
  blocking collectives  57.2 us (81%)
  Pallas kernels  11.4 us (16%)
    all_to_all x1, blocking collectives, local(): got = lax.all_to_all(send, 'dom', 0, 0)  35.3 us
    all_to_all x1, blocking collectives, local(): shares = lax.all_to_all(grads, 'ray', 0, 0)  12.4 us
    all_to_all x1, blocking collectives, local(): lax.all_to_all(jnp.broadcast_to(total[None], grads.shape), 'ray', 0, 0)  9.59 us
    pallas_call x1, Pallas kernels, local(): pl.pallas_call(forward_kernel, out_shape=(shape((ZONES, 2, 128), F32), sh...  5.41 us
    pallas_call x1, Pallas kernels, local(): pl.pallas_call(backward_kernel, out_shape=(shape((3, 1, OWN), F32), shape...  5.26 us

profile of v2, /device:TPU:6, one launch (start us, length us, event | category | flops | bytes accessed | tf_op | source)
XLA Modules:
  0.0 69.4 jit_solution(606865234854178594)
XLA Ops:
  0.6 5.4 %forward.1 = (f32[128,2,128]{2,1,0:T(2,128)S(1)}, bf16[64,4096]{1,0:T(8,128)(2,1)S(1)}, bf16[256,4096]{1,0:T(8,128)(2,1)S(1)}, bf16[256,4096]{1,0:T(8,128)(2,1)S...) custom-call(s32[1]{0:T(128)} %bitcast.part_ref, ...), custom_call_target="tpu_custom_call" | custom-call | tf_op jit(solution)/shard_map/forward/pallas_call | solution.py:302
  6.1 35.3 %all_to_all.15.got_ref = f32[128,2,128]{2,1,0:T(2,128)S(1)} all-to-all(f32[128,2,128]{2,1,0:T(2,128)S(1)} %get-tuple-element.19), channel_id=1, replica_groups=mesh['dom'=128,'ray'=4] {'dom'}, dimensions={0} | all-to-all | bytes 262144 | tf_op jit(solution)/shard_map/all_to_all | solution.py:339
  41.3 5.3 %backward.1 = (f32[3,1,4]{2,1,0:T(1,128)}, f32[4,88,256]{2,1,0:T(8,128)S(1)}) custom-call(s32[1]{0:T(128)} %bitcast.part_ref, f32[128,2,128]{2,1,0:T(2,128)S(1)} %all_to_all.15.got_ref, s32[1,8,128]{2,1,0:T(8,128)S(1)} %get-tuple-element.20.order_ref, f32[72,16]{1,0:T(8,128)S(1)} %get-tuple-element.21.reals_ref, f32[72,16]{1,0:T(8,128)S(1)} %get-tuple-element.22.whole_ref, ...), custom_call_target="tpu_custom_call" | custom-call | tf_op jit(solution)/shard_map/backward/pallas_call | solution.py:340
  46.6 12.4 %all_to_all.16 = f32[4,88,256]{2,1,0:T(8,128)S(1)} all-to-all(f32[4,88,256]{2,1,0:T(8,128)S(1)} %get-tuple-element.30), channel_id=1, replica_groups=mesh['dom'=128,'ray'=4] {'ray'}, dimensions={0} | all-to-all | bytes 720896 | tf_op jit(solution)/shard_map/all_to_all | solution.py:349
  59.0 9.6 %all_to_all.17.all_ref = f32[4,88,256]{2,1,0:T(8,128)S(1)} all-to-all(f32[4,88,256]{2,1,0:T(8,128)S(1)} %broadcast_in_dim.12), channel_id=1, replica_groups=mesh['dom'=128,'ray'=4] {'ray'}, dimensions={0} | all-to-all | bytes 720896 | tf_op jit(solution)/shard_map/all_to_all | solution.py:351
  68.6 0.7 %unpack.1 = (f32[63,1,256]{2,1,0:T(1,128)}, f32[256,256]{1,0:T(8,128)}, f32[4,256]{1,0:T(4,128)}) custom-call(f32[4,88,256]{2,1,0:T(8,128)S(1)} %all_to_all.17.all_ref), custom_call_target="tpu_custom_call" | custom-call | tf_op jit(solution)/shard_map/unpack/pallas_call | solution.py:352
  (2 shorter events, 0.0 us)

commit v3 on v1

v3 whole, which is shorter than its diff:
```python
import functools

import jax
import jax.numpy as jnp
from jax import lax
from jax.experimental import pallas as pl
from jax.experimental.pallas import tpu as pltpu
from jax.sharding import PartitionSpec as P

NFREQ = 10
FEATS = 63
S = 64
K = 4
NB = 8
CAP = 64
ZONES = 128
RG = 512
OWN = 4
ROWS = 32
SEL = 72
FIRST = 84
COLS = CAP * S
TILE = 16
CHUNK = 88
F32 = jnp.float32
BF16 = jnp.bfloat16


def iota(shape, dim):
    return lax.broadcasted_iota(jnp.int32, shape, dim)


def one_hot(mask):
    return mask.astype(F32).astype(BF16)


def split(x, terms):
    parts = []
    for _ in range(terms):
        parts.append(x.astype(BF16))
        x = x - parts[-1].astype(F32)
    return parts


def dot(a, b):
    return jnp.dot(a, b, preferred_element_type=F32)


def dot_nt(a, b):
    return lax.dot_general(a, b, (((1,), (1,)), ((), ())), preferred_element_type=F32)


def split_dot(x, exact):
    return sum(dot(part, exact) for part in split(x, 2))


def halves(column):
    lane = iota((ROWS, 2 * S), 1)
    return jnp.where(lane < S, column[0:ROWS], column[ROWS : 2 * ROWS])


def sin_cos(x):
    turns = jnp.floor(x * 0.6366197723675814 + 0.5)
    r = ((x - turns * 1.5703125) - turns * 4.837512969970703e-4) - turns * 7.54978995489188e-8
    z = r * r
    s = ((-1.9515295891e-4 * z + 8.3321608736e-3) * z - 1.6666654611e-1) * z * r + r
    c = ((2.443315711809948e-5 * z - 1.388731625493765e-3) * z + 4.166664568298827e-2) * z * z - 0.5 * z + 1.0
    quadrant = turns.astype(jnp.int32)
    swap = (quadrant & 1) == 1
    sin_r = jnp.where(swap, c, s)
    cos_r = jnp.where(swap, s, c)
    sin_r = jnp.where((quadrant & 2) == 2, -sin_r, sin_r)
    cos_r = jnp.where(((quadrant + 1) & 2) == 2, -cos_r, cos_r)
    return sin_r, cos_r


def shade(raw, step_d, count_d):
    index = iota(step_d.shape, 1) & (S - 1)
    scale = jnp.where(index.astype(F32) < count_d, step_d, 0.0)
    decay = jnp.exp(-jnp.abs(raw[0]))
    density = jnp.maximum(raw[0], 0.0) + jnp.log1p(decay)
    optical = density * scale
    source, target = iota((2 * S, 2 * S), 0), iota((2 * S, 2 * S), 1)
    upto = one_hot((source <= target) & ((source < S) == (target < S)))
    reached = split_dot(optical, upto)
    entering = jnp.exp(optical - reached)
    weight = entering - jnp.exp(-reached)
    albedo = [1.0 / (1.0 + jnp.exp(-raw[c])) for c in (1, 2, 3)]
    return scale, optical, entering, weight, albedo


def forward_kernel(
    part_ref, anchor_hbm, direct_hbm, entry_hbm, step_hbm, counts_hbm, crossing_hbm, target_hbm, order_hbm,
    w_in_hbm, w_mid_hbm, w_out_hbm,
    send_ref, enc_ref, one_ref, two_ref, pick_ref, low_ref, high_ref, info_ref, shade_ref, w_mid_t_ref, w_out_t_ref,
    anchor_ref, direct_ref, entry_ref, step_ref, counts_ref, crossing_ref, target_ref, order_ref,
    w_in_ref, w_mid_ref, w_out_ref, vals, ints, ranks, feats, raws, win, wout, sems,
):
    copies = [
        pltpu.make_async_copy(source, target, sems.at[i])
        for i, (source, target) in enumerate((
            (crossing_hbm, crossing_ref), (entry_hbm, entry_ref), (step_hbm, step_ref), (counts_hbm, counts_ref),
            (anchor_hbm, anchor_ref), (direct_hbm, direct_ref), (w_in_hbm, w_in_ref), (w_mid_hbm, w_mid_ref),
            (w_out_hbm, w_out_ref), (target_hbm, target_ref), (order_hbm, order_ref),
        ))
    ]
    for copy in copies:
        copy.start()
    part = part_ref[0]
    earlier = one_hot(iota((RG, RG), 0) < iota((RG, RG), 1))
    vals[...] = jnp.zeros_like(vals)
    ints[...] = jnp.zeros_like(ints)
    win[...] = jnp.zeros_like(win)
    wout[...] = jnp.zeros_like(wout)
    feats[FEATS * ROWS : (FEATS + 1) * ROWS] = jnp.zeros((ROWS, 2 * S), F32)
    for copy in copies:
        copy.wait()

    crossing = crossing_ref[0]
    own = crossing == part
    crossed = own[0:1] | own[1:2] | own[2:3] | own[3:4]
    place_own = dot(one_hot(jnp.broadcast_to(crossed, (16, RG))), earlier)[0:1]
    place_own = jnp.where(crossed, place_own.astype(jnp.int32), -1)
    row, ray = iota((SEL, RG), 0), iota((1, RG), 1)
    in_slot = (row < CAP) & (place_own == row)
    own_ray = (row >= CAP) & (row < CAP + OWN) & (ray == part * OWN + (row - CAP))
    selector = one_hot(in_slot | own_ray)

    def of_own(ref):
        return jnp.sum(jnp.where(own, ref[0].astype(F32), 0.0), axis=0, keepdims=True)

    for d in range(3):
        vals[d : d + 1] = anchor_ref[d]
        vals[3 + d : 4 + d] = direct_ref[d]
        vals[16 + d : 17 + d] = target_ref[d]
    vals[6:7] = of_own(entry_ref)
    vals[7:8] = of_own(step_ref)
    vals[8:9] = of_own(counts_ref)
    reals = sum(dot_nt(selector, piece) for piece in split(vals[0:16], 3))

    columns = [halves(reals[0:CAP, j : j + 1]) for j in range(9)]
    step_d, count_d = columns[7], columns[8]
    index = (iota((ROWS, 2 * S), 1) & (S - 1)).astype(F32)
    depth = columns[6] + (index + 0.5) * step_d
    for d in range(3):
        point = columns[d] + depth * columns[3 + d]
        feats[d * ROWS : (d + 1) * ROWS] = point
        sin_x, cos_x = sin_cos(point)
        for level in range(NFREQ):
            at = 3 + 6 * level + d
            feats[at * ROWS : (at + 1) * ROWS] = sin_x
            feats[(at + 3) * ROWS : (at + 4) * ROWS] = cos_x
            sin_x, cos_x = 2.0 * sin_x * cos_x, 1.0 - 2.0 * sin_x * sin_x

    win[0:FEATS] = w_in_ref[...].astype(F32)
    w_in = win[...].T.astype(BF16)
    w_mid = w_mid_ref[...]
    w_out = w_out_ref[...]
    half = one_hot(iota((8, 2 * S), 0) == iota((8, 2 * S), 1) // S)
    sent = []
    for tile in range(ROWS // TILE):
        span = slice(tile * TILE * 128, (tile + 1) * TILE * 128)
        encoded = jnp.concatenate(
            [feats[pl.ds(tile * TILE + j, FEATS + 1, stride=ROWS), :].astype(BF16) for j in range(TILE)], axis=1
        )
        enc_ref[:, span] = encoded
        one = jnp.maximum(dot(w_in, encoded), 0.0).astype(BF16)
        one_ref[:, span] = one
        two = jnp.maximum(dot(w_mid, one), 0.0).astype(BF16)
        two_ref[:, span] = two
        raw = dot(w_out, two)
        for j in range(TILE):
            raws[pl.ds(tile * TILE + j, 4, stride=ROWS), :] = raw[:, j * 128 : (j + 1) * 128]
        rows = slice(tile * TILE, (tile + 1) * TILE)
        raw = [raws[c * ROWS + tile * TILE : c * ROWS + (tile + 1) * TILE] for c in range(4)]
        scale, optical, entering, weight, albedo = shade(raw, step_d[rows], count_d[rows])
        sums = jnp.concatenate([weight * albedo[0], weight * albedo[1], weight * albedo[2], -optical], axis=0)
        sent.append(sum(dot_nt(half, piece) for piece in split(sums, 2)))
        kept = [entering, weight, scale / (1.0 + jnp.exp(-raw[0]))] + albedo
        kept = kept + [weight * a * (1.0 - a) for a in albedo]
        for i, value in enumerate(kept):
            shade_ref[i * ROWS + tile * TILE : i * ROWS + (tile + 1) * TILE] = value
    sent = jnp.concatenate(sent, axis=1)
    send_ref[...] = jnp.broadcast_to(sent[None, 0:2], send_ref.shape)

    zone = iota((ZONES, RG), 0)
    names = [zone == crossing[k : k + 1] for k in range(K)]
    ranks[...] = dot(one_hot(names[0] | names[1] | names[2] | names[3]), earlier)
    place_all = ranks[...]
    ints[0:4] = crossing.astype(F32)
    for k in range(K):
        ints[4 + k : 5 + k] = jnp.sum(jnp.where(names[k], place_all, 0.0), axis=0, keepdims=True)
    ints[8:9] = (ray // (RG // NB)).astype(F32)
    ints[9:10] = jnp.ones((1, RG), F32)
    whole = ints[...].astype(BF16)
    table = dot_nt(selector, whole)
    info_ref[0:16] = dot_nt(whole, selector)
    info_ref[16:24] = sum(dot_nt(piece, selector) for piece in split(vals[16:24], 3))
    bundle = one_hot(table[:, 8:9].astype(jnp.int32) == iota((SEL, NB), 1))
    order = dot(bundle, order_ref[0].astype(F32).astype(BF16))
    lane = iota((SEL, ZONES), 1)
    lister = ((lane + FIRST) & (ZONES - 1)).astype(F32)
    positions = iota((8, ZONES), 1).astype(F32).astype(BF16)
    for k in range(K):
        named = table[:, k : k + 1]
        place = table[:, 4 + k : 5 + k].astype(jnp.int32)
        pick_ref[k * SEL : (k + 1) * SEL] = one_hot(named == lister)
        wanted = ((lane & 15) == (place & 15)) & ((lane >> 6) == ((place >> 4) & 1))
        low_ref[k * SEL : (k + 1) * SEL] = (wanted & (place < ROWS)).astype(F32)
        high_ref[k * SEL : (k + 1) * SEL] = (wanted & (place >= ROWS)).astype(F32)
        info_ref[24 + k : 25 + k] = dot_nt(positions, one_hot(order == named))[0:1]
    info_ref[28:32] = jnp.zeros((4, SEL), F32)
    wout[0:4] = w_out.astype(F32)
    w_out_t_ref[...] = wout[...].T.astype(BF16)
    w_mid_t_ref[...] = w_mid.astype(F32).T.astype(BF16)


def backward_kernel(
    part_ref, got_ref, pick_ref, low_ref, high_ref, info_ref, shade_ref, enc_ref, one_ref, two_ref,
    w_mid_t_ref, w_out_t_ref,
    rendered_ref, grads_ref,
    draw,
):
    part = part_ref[0].astype(F32)
    pieces = split(jnp.concatenate([got_ref[:, 0, :], got_ref[:, 1, :]], axis=1), 2)
    gather = one_hot(iota((8, ZONES), 0) == ((iota((8, ZONES), 1) >> 4) & 3))
    pick = pick_ref[...]
    low, high = low_ref[...] > 0.5, high_ref[...] > 0.5
    values = jnp.zeros((8, K * SEL), F32)
    for piece in pieces:
        both = dot(pick, piece)
        found = jnp.where(low, both[:, 0:128], jnp.where(high, both[:, 128:256], 0.0))
        values = values + dot_nt(gather, found.astype(BF16))

    mine = [values[:, k * SEL : (k + 1) * SEL] for k in range(K)]
    log = [mine[k][3:4] for k in range(K)]
    color = [mine[k][0:3] for k in range(K)]
    named = [info_ref[k : k + 1] for k in range(K)]
    used = info_ref[9:10] > 0.5
    goal = info_ref[16:19]
    rank = [info_ref[24 + k : 25 + k] for k in range(K)]
    fade = [
        jnp.exp(sum(jnp.where(rank[j] < rank[k], log[j], 0.0) for j in range(K) if j != k)) for k in range(K)
    ]
    clear = jnp.exp(log[0] + log[1] + log[2] + log[3])
    rendered = sum(fade[k] * color[k] for k in range(K)) + clear
    residual = rendered - goal
    share = [fade[k] * jnp.sum(residual * color[k], axis=0, keepdims=True) for k in range(K)]
    owned = [named[k] == part for k in range(K)]
    own_rank = sum(jnp.where(owned[k], rank[k], 0.0) for k in range(K))
    own_fade = sum(jnp.where(owned[k], fade[k], 0.0) for k in range(K))
    dlog = sum(jnp.where(rank[k] > own_rank, share[k], 0.0) for k in range(K))
    dlog = dlog + clear * jnp.sum(residual, axis=0, keepdims=True)
    dcolor = own_fade * residual
    for c in range(3):
        rendered_ref[c] = rendered[c : c + 1, CAP : CAP + OWN]
    slots = jnp.concatenate([dcolor, dlog, jnp.zeros((4, SEL), F32)], axis=0)
    slots = jnp.where(used, slots, 0.0)
    slots = jnp.concatenate([slots, jnp.zeros((8, 128 - SEL), F32)], axis=1).T

    entering, weight, slope, *rest = [shade_ref[i * ROWS : (i + 1) * ROWS] for i in range(9)]
    dcolor_d = [halves(slots[0:CAP, c : c + 1]) for c in range(3)]
    gain = sum(dcolor_d[c] * rest[c] for c in range(3))
    source, target = iota((2 * S, 2 * S), 0), iota((2 * S, 2 * S), 1)
    since = one_hot((source >= target) & ((source < S) == (target < S)))
    behind = split_dot(gain * weight, since)
    draw[0:ROWS] = (gain * entering - behind - halves(slots[0:CAP, 3:4])) * slope
    for c in range(3):
        draw[(c + 1) * ROWS : (c + 2) * ROWS] = dcolor_d[c] * rest[3 + c]
    draw[4 * ROWS :] = jnp.zeros((12 * ROWS, 2 * S), F32)

    w_out_t, w_mid_t = w_out_t_ref[...], w_mid_t_ref[...]
    grad_out = jnp.zeros((16, 256), F32)
    grad_mid = jnp.zeros((256, 256), F32)
    grad_in = jnp.zeros((256, 64), F32)
    zero = jnp.zeros((), BF16)
    for tile in range(ROWS // TILE):
        span = slice(tile * TILE * 128, (tile + 1) * TILE * 128)
        low = jnp.concatenate(
            [draw[pl.ds(tile * TILE + j, 16, stride=ROWS), :].astype(BF16) for j in range(TILE)], axis=1
        )
        two, one = two_ref[:, span], one_ref[:, span]
        grad_out = grad_out + dot_nt(low, two)
        d_two = jnp.where(two > 0, dot(w_out_t, low).astype(BF16), zero)
        grad_mid = grad_mid + dot_nt(d_two, one)
        d_one = jnp.where(one > 0, dot(w_mid_t, d_two).astype(BF16), zero)
        grad_in = grad_in + dot_nt(d_one, enc_ref[:, span])
    grad_in = grad_in.T
    for q in range(4):
        grads_ref[q, 0:64] = grad_mid[64 * q : 64 * q + 64]
        grads_ref[q, 64:80] = grad_in[16 * q : 16 * q + 16]
        grads_ref[q, 80:88] = jnp.broadcast_to(grad_out[q : q + 1], (8, 256))


def unpack_kernel(all_ref, in_ref, mid_ref, out_ref):
    for q in range(4):
        mid_ref[64 * q : 64 * q + 64] = all_ref[q, 0:64]
        rows = min(16, FEATS - 16 * q)
        in_ref[16 * q : 16 * q + rows, 0, :] = all_ref[q, 64 : 64 + rows]
        out_ref[q : q + 1] = all_ref[q, 80:81]


def vmem(count):
    return [pl.BlockSpec(memory_space=pltpu.VMEM)] * count


def in_hbm(array):
    return pltpu.with_memory_space_constraint(array, pltpu.HBM)


def local(anchor, direct, entry, step, counts, crossing, order, target, w_in, w_mid, w_out):
    part = lax.axis_index("dom").astype(jnp.int32).reshape(1)
    entry, step, counts, crossing = (jnp.swapaxes(a, 1, 2) for a in (entry, step, counts, crossing))
    w_in_t = jnp.swapaxes(w_in, 1, 2)[0]
    scalar = pl.BlockSpec(memory_space=pltpu.SMEM)
    params = pltpu.CompilerParams(vmem_limit_bytes=40 * 1024 * 1024)
    shape = jax.ShapeDtypeStruct
    arguments = [in_hbm(a) for a in (
        anchor, direct, entry, step, counts, crossing, target, order, w_in_t, w_mid[0], w_out[0]
    )]
    send, *kept = pl.pallas_call(
        forward_kernel,
        out_shape=(
            shape((ZONES, 2, 128), F32),
            shape((64, COLS), BF16),
            shape((256, COLS), BF16),
            shape((256, COLS), BF16),
            shape((K * SEL, ZONES), BF16),
            shape((K * SEL, ZONES), F32),
            shape((K * SEL, ZONES), F32),
            shape((32, SEL), F32),
            shape((9 * ROWS, 128), F32),
            shape((256, 256), BF16),
            shape((256, 16), BF16),
        ),
        in_specs=[scalar] + [pl.BlockSpec(memory_space=pltpu.HBM)] * 11,
        out_specs=vmem(11),
        scratch_shapes=[pltpu.VMEM(a.shape, a.dtype) for a in arguments]
        + [
            pltpu.VMEM((24, RG), F32),
            pltpu.VMEM((16, RG), F32),
            pltpu.VMEM((ZONES, RG), F32),
            pltpu.VMEM((64 * ROWS, 128), F32),
            pltpu.VMEM((4 * ROWS, 128), F32),
            pltpu.VMEM((64, 256), F32),
            pltpu.VMEM((16, 256), F32),
            pltpu.SemaphoreType.DMA((11,)),
        ],
        compiler_params=params,
        name="forward",
    )(part, *arguments)
    listed = [[(i + FIRST) % ZONES for i in range(ZONES)]]
    got = lax.all_to_all(send, "dom", 0, 0, axis_index_groups=listed)
    enc, one, two, pick, low, high, info, shaded, w_mid_t, w_out_t = kept
    rendered, grads = pl.pallas_call(
        backward_kernel,
        out_shape=(shape((3, 1, OWN), F32), shape((4, CHUNK, 256), F32)),
        in_specs=[scalar] + vmem(11),
        out_specs=vmem(2),
        scratch_shapes=[pltpu.VMEM((16 * ROWS, 128), F32)],
        compiler_params=params,
        name="backward",
    )(part, got, pick, low, high, info, shaded, enc, one, two, w_mid_t, w_out_t)
    shares = lax.all_to_all(grads, "ray", 0, 0)
    total = jnp.sum(shares, axis=0)
    everything = lax.all_to_all(jnp.broadcast_to(total[None], grads.shape), "ray", 0, 0)
    grad_i, grad_m, grad_o = pl.pallas_call(
        unpack_kernel,
        out_shape=(shape((FEATS, 1, 256), F32), shape((256, 256), F32), shape((4, 256), F32)),
        in_specs=vmem(1),
        out_specs=vmem(3),
        compiler_params=params,
        name="unpack",
    )(everything)
    return rendered, jnp.transpose(grad_i, (1, 2, 0)), grad_m[None], grad_o[None]


def solution(mesh):
    in_specs = (
        P(None, "ray", None),
        P(None, "ray", None),
        P("ray", None, None),
        P("ray", None, None),
        P("ray", None, None),
        P("ray", None, None),
        P("ray", None, None),
        P(None, "ray", None),
        P("dom", None, None),
        P("dom", None, None),
        P("dom", None, None),
    )
    out_specs = (
        P(None, "ray", "dom"),
        P("dom", None, None),
        P("dom", None, None),
        P("dom", None, None),
    )
    return jax.shard_map(local, mesh=mesh, in_specs=in_specs, out_specs=out_specs, check_vma=False)
```

time: 78.5 us -> 62.3 us (0.79); the launches traced: 77.2 us -> 62 us
  local copies, waits for them, and re-layouts: 8.81 us -> 0.03 us
  blocking collectives: 57.2 us -> 51.7 us
  Pallas kernels: 10.5 us -> 9.62 us
    unnamed x24 -> x0, local copies, waits for them, and re-layouts: 8.79 us -> none
    all_to_all x1, blocking collectives: 35.3 us -> 29.8 us  [local(): got = lax.all_to_all(send, 'dom', 0, 0, axis_index_groups=listed)]
    pallas_call x1, Pallas kernels: 5.2 us -> 4 us  [local(): pl.pallas_call(backward_kernel, out_shape=(shape((3, 1, OWN), F32), shape...]
where the time goes in v3:
time: 62.3 us; the launch traced here: 62 us
  blocking collectives  51.7 us (83%)
  Pallas kernels  9.62 us (15%)
  between operations  0.67 us (1%)
    all_to_all x1, blocking collectives, local(): got = lax.all_to_all(send, 'dom', 0, 0, axis_index_groups=listed)  29.8 us
    all_to_all x1, blocking collectives, local(): shares = lax.all_to_all(grads, 'ray', 0, 0)  12.3 us
    all_to_all x1, blocking collectives, local(): lax.all_to_all(jnp.broadcast_to(total[None], grads.shape), 'ray', 0, 0)  9.59 us
    pallas_call x1, Pallas kernels, local(): pl.pallas_call(forward_kernel, out_shape=(shape((ZONES, 2, 128), F32), sh...  4.88 us
    pallas_call x1, Pallas kernels, local(): pl.pallas_call(backward_kernel, out_shape=(shape((3, 1, OWN), F32), shape...  4 us

profile of v3, /device:TPU:6, one launch (start us, length us, event | category | flops | bytes accessed | tf_op | source)
XLA Modules:
  0.0 62.0 jit_solution(3530254284267176665)
XLA Ops:
  0.6 4.9 %forward.1 = (f32[128,2,128]{2,1,0:T(2,128)S(1)}, bf16[64,4096]{1,0:T(8,128)(2,1)S(1)}, bf16[256,4096]{1,0:T(8,128)(2,1)S(1)}, bf16[256,4096]{1,0:T(8,128)(2,1)S...) custom-call(s32[1]{0:T(128)} %bitcast.part_ref, ...), custom_call_target="tpu_custom_call" | custom-call | tf_op jit(solution)/shard_map/forward/pallas_call | solution.py:321
  5.5 29.8 %all_to_all.15.got_ref = f32[128,2,128]{2,1,0:T(2,128)S(1)} all-to-all(f32[128,2,128]{2,1,0:T(2,128)S(1)} %get-tuple-element.20), channel_id=1, replica_groups={{336,340,344,348,352,356,360,364,368,372,376,380,384,388,392,396,400,40..., dimensions={0} | all-to-all | bytes 262144 | tf_op jit(solution)/shard_map/all_to_all | solution.py:353
  35.4 4.0 %backward.1 = (f32[3,1,4]{2,1,0:T(1,128)}, f32[4,88,256]{2,1,0:T(8,128)S(1)}) custom-call(s32[1]{0:T(128)} %bitcast.part_ref, f32[128,2,128]{2,1,0:T(2,128)S(1)} %all_to_all.15.got_ref, bf16[288,128]{1,0:T(8,128)(2,1)S(1)} %get-tuple-element.21.pick_ref, f32[288,128]{1,0:T(8,128)S(1)} %get-tuple-element.22.low_ref, ...), custom_call_target="tpu_custom_call" | custom-call | tf_op jit(solution)/shard_map/backward/pallas_call | solution.py:355
  39.4 12.3 %all_to_all.16 = f32[4,88,256]{2,1,0:T(8,128)S(1)} all-to-all(f32[4,88,256]{2,1,0:T(8,128)S(1)} %get-tuple-element.32), channel_id=1, replica_groups=mesh['dom'=128,'ray'=4] {'ray'}, dimensions={0} | all-to-all | bytes 720896 | tf_op jit(solution)/shard_map/all_to_all | solution.py:364
  51.7 9.6 %all_to_all.17.all_ref = f32[4,88,256]{2,1,0:T(8,128)S(1)} all-to-all(f32[4,88,256]{2,1,0:T(8,128)S(1)} %broadcast_in_dim.12), channel_id=1, replica_groups=mesh['dom'=128,'ray'=4] {'ray'}, dimensions={0} | all-to-all | bytes 720896 | tf_op jit(solution)/shard_map/all_to_all | solution.py:366
  61.3 0.7 %unpack.1 = (f32[63,1,256]{2,1,0:T(1,128)}, f32[256,256]{1,0:T(8,128)}, f32[4,256]{1,0:T(4,128)}) custom-call(f32[4,88,256]{2,1,0:T(8,128)S(1)} %all_to_all.17.all_ref), custom_call_target="tpu_custom_call" | custom-call | tf_op jit(solution)/shard_map/unpack/pallas_call | solution.py:367
  (2 shorter events, 0.0 us)

commit v4 on v3

--- a/solution.py
+++ b/solution.py
@@ -199,7 +199,8 @@
     bundle = one_hot(table[:, 8:9].astype(jnp.int32) == iota((SEL, NB), 1))
     order = dot(bundle, order_ref[0].astype(F32).astype(BF16))
     lane = iota((SEL, ZONES), 1)
-    lister = ((lane + FIRST) & (ZONES - 1)).astype(F32)
+    lister = ((2 * lane + FIRST) & (ZONES - 1)) + jnp.where(lane < ZONES // 2, part & 1, 1 - (part & 1))
+    lister = lister.astype(F32)
     positions = iota((8, ZONES), 1).astype(F32).astype(BF16)
     for k in range(K):
         named = table[:, k : k + 1]
@@ -216,13 +217,14 @@
 
 
 def backward_kernel(
-    part_ref, got_ref, pick_ref, low_ref, high_ref, info_ref, shade_ref, enc_ref, one_ref, two_ref,
+    part_ref, near_ref, other_ref, pick_ref, low_ref, high_ref, info_ref, shade_ref, enc_ref, one_ref, two_ref,
     w_mid_t_ref, w_out_t_ref,
     rendered_ref, grads_ref,
     draw,
 ):
     part = part_ref[0].astype(F32)
-    pieces = split(jnp.concatenate([got_ref[:, 0, :], got_ref[:, 1, :]], axis=1), 2)
+    got = [jnp.concatenate([near_ref[:, h, :], other_ref[:, h, :]], axis=0) for h in range(2)]
+    pieces = split(jnp.concatenate(got, axis=1), 2)
     gather = one_hot(iota((8, ZONES), 0) == ((iota((8, ZONES), 1) >> 4) & 3))
     pick = pick_ref[...]
     low, high = low_ref[...] > 0.5, high_ref[...] > 0.5
@@ -321,7 +323,7 @@
     send, *kept = pl.pallas_call(
         forward_kernel,
         out_shape=(
-            shape((ZONES, 2, 128), F32),
+            shape((ZONES // 2, 2, 128), F32),
             shape((64, COLS), BF16),
             shape((256, COLS), BF16),
             shape((256, COLS), BF16),
@@ -349,21 +351,22 @@
         compiler_params=params,
         name="forward",
     )(part, *arguments)
-    listed = [[(i + FIRST) % ZONES for i in range(ZONES)]]
-    got = lax.all_to_all(send, "dom", 0, 0, axis_index_groups=listed)
+    listed = [[(2 * i + FIRST) % ZONES + core for i in range(ZONES // 2)] for core in range(2)]
+    near = lax.all_to_all(send, "dom", 0, 0, axis_index_groups=listed)
+    other = lax.ppermute(near, "dom", [(i, i ^ 1) for i in range(ZONES)])
     enc, one, two, pick, low, high, info, shaded, w_mid_t, w_out_t = kept
     rendered, grads = pl.pallas_call(
         backward_kernel,
         out_shape=(shape((3, 1, OWN), F32), shape((4, CHUNK, 256), F32)),
-        in_specs=[scalar] + vmem(11),
+        in_specs=[scalar] + vmem(12),
         out_specs=vmem(2),
         scratch_shapes=[pltpu.VMEM((16 * ROWS, 128), F32)],
         compiler_params=params,
         name="backward",
-    )(part, got, pick, low, high, info, shaded, enc, one, two, w_mid_t, w_out_t)
-    shares = lax.all_to_all(grads, "ray", 0, 0)
+    )(part, near, other, pick, low, high, info, shaded, enc, one, two, w_mid_t, w_out_t)
+    shares = lax.all_to_all(grads, "ray", 0, 0, axis_index_groups=[[2, 1, 0, 3]])
     total = jnp.sum(shares, axis=0)
-    everything = lax.all_to_all(jnp.broadcast_to(total[None], grads.shape), "ray", 0, 0)
+    everything = lax.all_to_all(jnp.broadcast_to(total[None], grads.shape), "ray", 0, 0, axis_index_groups=[[2, 1, 0, 3]])
     grad_i, grad_m, grad_o = pl.pallas_call(
         unpack_kernel,
         out_shape=(shape((FEATS, 1, 256), F32), shape((256, 256), F32), shape((4, 256), F32)),

time: 62.3 us -> 60.2 us (0.966)
  blocking collectives: 51.7 us -> 46.4 us
  starting transfers between devices: 0 us -> 1.91 us
  waiting for transfers between devices: 0 us -> 1.22 us
    all_to_all x3, blocking collectives: 51.7 us -> 46.4 us  [the longest x1 25.6 us: local(): near = lax.all_to_all(send, 'dom', 0, 0, axis_index_groups=listed)]
    ppermute x0 -> x1, starting transfers between devices: none -> 1.91 us  [local(): other = lax.ppermute(near, 'dom', [(i, i ^ 1) for i in range(ZONES)])]
    ppermute x0 -> x1, waiting for transfers between devices: none -> 1.22 us  [local(): other = lax.ppermute(near, 'dom', [(i, i ^ 1) for i in range(ZONES)])]
  transfers between devices with their start and end apart: 0 -> 1, of which waited for: 0 -> 1; matrix products, arithmetic and copies ran while one was open for 0% -> 0% of each run, Pallas kernels for 0% -> 0%
where the time goes in v4:
time: 60.2 us; the launch traced here: 59.9 us
  blocking collectives  46.4 us (77%)
  Pallas kernels  9.6 us (16%)
  starting transfers between devices  1.91 us (3%)
  waiting for transfers between devices  1.22 us (2%)
  between operations  0.68 us (1%)
    all_to_all x1, blocking collectives, local(): near = lax.all_to_all(send, 'dom', 0, 0, axis_index_groups=listed)  25.6 us
    all_to_all x1, blocking collectives, local(): lax.all_to_all(grads, 'ray', 0, 0, axis_index_groups=[[2, 1, 0, 3]])  10.9 us
    all_to_all x1, blocking collectives, local(): lax.all_to_all(jnp.broadcast_to(total[None], grads.shape), 'ray', 0, 0, a...  9.88 us
    pallas_call x1, Pallas kernels, local(): pl.pallas_call(forward_kernel, out_shape=(shape((ZONES // 2, 2, 128), F32...  4.87 us
    pallas_call x1, Pallas kernels, local(): pl.pallas_call(backward_kernel, out_shape=(shape((3, 1, OWN), F32), shape...  3.99 us
    ppermute x1, starting transfers between devices, local(): other = lax.ppermute(near, 'dom', [(i, i ^ 1) for i in range(ZONES)])  1.91 us
    ppermute x1, waiting for transfers between devices, local(): other = lax.ppermute(near, 'dom', [(i, i ^ 1) for i in range(ZONES)])  1.22 us
  transfers between devices with their start and end apart: 1, of which 1 were waited for; matrix products, arithmetic and copies ran while one was open for 0% of the time, Pallas kernels for 0%

profile of v4, /device:TPU:6, one launch (start us, length us, event | category | flops | bytes accessed | tf_op | source)
XLA Modules:
  0.0 59.9 jit_solution(10348127874680786373)
XLA Ops:
  0.6 4.9 %forward.1 = (f32[64,2,128]{2,1,0:T(2,128)S(1)}, bf16[64,4096]{1,0:T(8,128)(2,1)S(1)}, bf16[256,4096]{1,0:T(8,128)(2,1)S(1)}, bf16[256,4096]{1,0:T(8,128)(2,1)S(...) custom-call(s32[1]{0:T(128)} %bitcast.part_ref, ...), custom_call_target="tpu_custom_call" | custom-call | tf_op jit(solution)/shard_map/forward/pallas_call | solution.py:323
  5.5 25.6 %all_to_all.15.near_ref = f32[64,2,128]{2,1,0:T(2,128)S(1)} all-to-all(f32[64,2,128]{2,1,0:T(2,128)S(1)} %get-tuple-element.20), channel_id=1, replica_groups={{336,344,352,360,368,376,384,392,400,408,416,424,432,440,448,456,464,47..., dimensions={0} | all-to-all | bytes 131072 | tf_op jit(solution)/shard_map/all_to_all | solution.py:355
  31.1 1.9 %collective-permute-start = (f32[64,2,128]{2,1,0:T(2,128)S(1)}, f32[64,2,128]{2,1,0:T(2,128)S(1)}, u32[]{:S(2)}, u32[]{:S(2)}) collective-permute-start(f32[64,2,128]{2,1,0:T(2,128)S(1)} %all_to_all.15.near_ref), channel_id=1, source_target_pairs={{0,4},{4,0},{8,12},{12,8},{16,20},{20,16},{24,28},{28,24},{32,36},... | collective-permute-start | bytes 196616 | tf_op jit(solution)/shard_map/ppermute | solution.py:356
  33.1 1.2 %collective-permute-done.other_ref = f32[64,2,128]{2,1,0:T(2,128)S(1)} collective-permute-done((f32[64,2,128]{2,1,0:T(2,128)S(1)}, f32[64,2,128]{2,1,0:T(2,128)S(1)}, u32[]{:S(2)}, u32[]{:S(2)}) %collective-permute-start) | collective-permute-done | bytes 65568 | tf_op jit(solution)/shard_map/ppermute | solution.py:356
  34.3 4.0 %backward.1 = (f32[3,1,4]{2,1,0:T(1,128)}, f32[4,88,256]{2,1,0:T(8,128)S(1)}) custom-call(s32[1]{0:T(128)} %bitcast.part_ref, f32[64,2,128]{2,1,0:T(2,128)S(1)} %all_to_all.15.near_ref, f32[64,2,128]{2,1,0:T(2,128)S(1)} %collective-permute-done.other_ref, bf16[288,128]{1,0:T(8,128)(2,1)S(1)} %get-tuple-element.21.pick_ref, ...), custom_call_target="tpu_custom_call" | custom-call | tf_op jit(solution)/shard_map/backward/pallas_call | solution.py:358
  38.3 10.9 %all_to_all.16 = f32[4,88,256]{2,1,0:T(8,128)S(1)} all-to-all(f32[4,88,256]{2,1,0:T(8,128)S(1)} %get-tuple-element.32), channel_id=1, replica_groups={{2,1,0,3},{6,5,4,7},{10,9,8,11},{14,13,12,15},{18,17,16,19},{22,21,20,2..., dimensions={0} | all-to-all | bytes 720896 | tf_op jit(solution)/shard_map/all_to_all | solution.py:367
  49.3 9.9 %all_to_all.17.all_ref = f32[4,88,256]{2,1,0:T(8,128)S(1)} all-to-all(f32[4,88,256]{2,1,0:T(8,128)S(1)} %broadcast_in_dim.12), channel_id=1, replica_groups={{2,1,0,3},{6,5,4,7},{10,9,8,11},{14,13,12,15},{18,17,16,19},{22,21,20,2..., dimensions={0} | all-to-all | bytes 720896 | tf_op jit(solution)/shard_map/all_to_all | solution.py:369
  59.2 0.7 %unpack.1 = (f32[63,1,256]{2,1,0:T(1,128)}, f32[256,256]{1,0:T(8,128)}, f32[4,256]{1,0:T(4,128)}) custom-call(f32[4,88,256]{2,1,0:T(8,128)S(1)} %all_to_all.17.all_ref), custom_call_target="tpu_custom_call" | custom-call | tf_op jit(solution)/shard_map/unpack/pallas_call | solution.py:370
  (2 shorter events, 0.0 us)
Async XLA Ops:
  31.1 3.1 %collective-permute-start = (f32[64,2,128]{2,1,0:T(2,128)S(1)}, f32[64,2,128]{2,1,0:T(2,128)S(1)}, u32[]{:S(2)}, u32[]{:S(2)}) collective-permute-start(f32[64,2,128]{2,1,0:T(2,128)S(1)} %all_to_all.15.near_ref), channel_id=1, source_target_pairs={{0,4},{4,0},{8,12},{12,8},{16,20},{20,16},{24,28},{28,24},{32,36},... | collective-permute-start | bytes 196616 | tf_op jit(solution)/shard_map/ppermute | solution.py:356

commit v5 on v4

--- a/solution.py
+++ b/solution.py
@@ -2,6 +2,7 @@
 
 import jax
 import jax.numpy as jnp
+import numpy as np
 from jax import lax
 from jax.experimental import pallas as pl
 from jax.experimental.pallas import tpu as pltpu
@@ -19,11 +20,23 @@
 ROWS = 32
 SEL = 72
 FIRST = 84
+EARLY = 48
+SPAN = (16, 4)
 COLS = CAP * S
 TILE = 16
 CHUNK = 88
 F32 = jnp.float32
 BF16 = jnp.bfloat16
+
+
+def listing():
+    def far(index):
+        hops = 0
+        for place, first, length in zip(divmod(index // 2, SPAN[1]), divmod(FIRST // 2, SPAN[1]), SPAN):
+            hops += min((place - first) % length, (first - place) % length)
+        return index // 2 != FIRST // 2, -hops
+
+    return [sorted(range(core, ZONES, 2), key=far) for core in range(2)]
 
 
 def iota(shape, dim):
@@ -89,12 +102,69 @@
     return scale, optical, entering, weight, albedo
 
 
+def select(part, crossing):
+    earlier = one_hot(iota((RG, RG), 0) < iota((RG, RG), 1))
+    own = crossing == part
+    crossed = own[0:1] | own[1:2] | own[2:3] | own[3:4]
+    place_own = dot(one_hot(jnp.broadcast_to(crossed, (16, RG))), earlier)[0:1]
+    place_own = jnp.where(crossed, place_own.astype(jnp.int32), -1)
+    row, ray = iota((SEL, RG), 0), iota((1, RG), 1)
+    in_slot = (row < CAP) & (place_own == row)
+    own_ray = (row >= CAP) & (row < CAP + OWN) & (ray == part * OWN + (row - CAP))
+    return own, one_hot(in_slot | own_ray), earlier
+
+
+def prepare(
+    part, crossing_ref, target_ref, order_ref, lists_ref, w_mid_ref, w_out_ref,
+    pick_ref, low_ref, high_ref, info_ref, w_mid_t_ref, w_out_t_ref, ints, goals, ranks, wout,
+):
+    crossing = crossing_ref[0]
+    _, selector, earlier = select(part, crossing)
+    ray = iota((1, RG), 1)
+    ints[...] = jnp.zeros_like(ints)
+    goals[...] = jnp.zeros_like(goals)
+    for d in range(3):
+        goals[d : d + 1] = target_ref[d]
+    zone = iota((ZONES, RG), 0)
+    names = [zone == crossing[k : k + 1] for k in range(K)]
+    ranks[...] = dot(one_hot(names[0] | names[1] | names[2] | names[3]), earlier)
+    place_all = ranks[...]
+    ints[0:4] = crossing.astype(F32)
+    for k in range(K):
+        ints[4 + k : 5 + k] = jnp.sum(jnp.where(names[k], place_all, 0.0), axis=0, keepdims=True)
+    ints[8:9] = (ray // (RG // NB)).astype(F32)
+    ints[9:10] = jnp.ones((1, RG), F32)
+    whole = ints[...].astype(BF16)
+    table = dot_nt(selector, whole)
+    info_ref[0:16] = dot_nt(whole, selector)
+    info_ref[16:24] = sum(dot_nt(piece, selector) for piece in split(goals[...], 3))
+    bundle = one_hot(table[:, 8:9].astype(jnp.int32) == iota((SEL, NB), 1))
+    order = dot(bundle, order_ref[0].astype(F32).astype(BF16))
+    lane = iota((SEL, ZONES), 1)
+    lister = jnp.where((part & 1) == 0, lists_ref[0:1], lists_ref[1:2])
+    positions = iota((8, ZONES), 1).astype(F32).astype(BF16)
+    for k in range(K):
+        named = table[:, k : k + 1]
+        place = table[:, 4 + k : 5 + k].astype(jnp.int32)
+        pick_ref[k * SEL : (k + 1) * SEL] = one_hot(named == lister)
+        wanted = (lane & (ROWS - 1)) == (place & (ROWS - 1))
+        low_ref[k * SEL : (k + 1) * SEL] = (wanted & (place < ROWS)).astype(F32)
+        high_ref[k * SEL : (k + 1) * SEL] = (wanted & (place >= ROWS)).astype(F32)
+        info_ref[24 + k : 25 + k] = dot_nt(positions, one_hot(order == named))[0:1]
+    info_ref[28:32] = jnp.zeros((4, SEL), F32)
+    wout[...] = jnp.zeros_like(wout)
+    wout[0:4] = w_out_ref[...].astype(F32)
+    w_out_t_ref[...] = wout[...].T.astype(BF16)
+    w_mid_t_ref[...] = w_mid_ref[...].astype(F32).T.astype(BF16)
+
+
 def forward_kernel(
     part_ref, anchor_hbm, direct_hbm, entry_hbm, step_hbm, counts_hbm, crossing_hbm, target_hbm, order_hbm,
-    w_in_hbm, w_mid_hbm, w_out_hbm,
-    send_ref, enc_ref, one_ref, two_ref, pick_ref, low_ref, high_ref, info_ref, shade_ref, w_mid_t_ref, w_out_t_ref,
-    anchor_ref, direct_ref, entry_ref, step_ref, counts_ref, crossing_ref, target_ref, order_ref,
-    w_in_ref, w_mid_ref, w_out_ref, vals, ints, ranks, feats, raws, win, wout, sems,
+    w_in_hbm, w_mid_hbm, w_out_hbm, lists_hbm,
+    send_ref, enc_ref, one_ref, two_ref, shade_ref, crossing_ref, target_ref, order_ref, lists_ref, w_mid_ref, w_out_ref,
+    pick_ref, low_ref, high_ref, info_ref, w_mid_t_ref, w_out_t_ref,
+    anchor_ref, direct_ref, entry_ref, step_ref, counts_ref, w_in_ref, vals, feats, raws, win,
+    ints, goals, ranks, wout, sems,
 ):
     copies = [
         pltpu.make_async_copy(source, target, sems.at[i])
@@ -102,29 +172,22 @@
             (crossing_hbm, crossing_ref), (entry_hbm, entry_ref), (step_hbm, step_ref), (counts_hbm, counts_ref),
             (anchor_hbm, anchor_ref), (direct_hbm, direct_ref), (w_in_hbm, w_in_ref), (w_mid_hbm, w_mid_ref),
             (w_out_hbm, w_out_ref), (target_hbm, target_ref), (order_hbm, order_ref),
+            (lists_hbm, lists_ref),
         ))
     ]
     for copy in copies:
         copy.start()
     part = part_ref[0]
-    earlier = one_hot(iota((RG, RG), 0) < iota((RG, RG), 1))
     vals[...] = jnp.zeros_like(vals)
-    ints[...] = jnp.zeros_like(ints)
     win[...] = jnp.zeros_like(win)
     wout[...] = jnp.zeros_like(wout)
     feats[FEATS * ROWS : (FEATS + 1) * ROWS] = jnp.zeros((ROWS, 2 * S), F32)
-    for copy in copies:
+    copies[0].wait()
+
+    crossing = crossing_ref[0]
+    own, selector, _ = select(part, crossing)
+    for copy in copies[1:]:
         copy.wait()
-
-    crossing = crossing_ref[0]
-    own = crossing == part
-    crossed = own[0:1] | own[1:2] | own[2:3] | own[3:4]
-    place_own = dot(one_hot(jnp.broadcast_to(crossed, (16, RG))), earlier)[0:1]
-    place_own = jnp.where(crossed, place_own.astype(jnp.int32), -1)
-    row, ray = iota((SEL, RG), 0), iota((1, RG), 1)
-    in_slot = (row < CAP) & (place_own == row)
-    own_ray = (row >= CAP) & (row < CAP + OWN) & (ray == part * OWN + (row - CAP))
-    selector = one_hot(in_slot | own_ray)
 
     def of_own(ref):
         return jnp.sum(jnp.where(own, ref[0].astype(F32), 0.0), axis=0, keepdims=True)
@@ -132,11 +195,10 @@
     for d in range(3):
         vals[d : d + 1] = anchor_ref[d]
         vals[3 + d : 4 + d] = direct_ref[d]
-        vals[16 + d : 17 + d] = target_ref[d]
     vals[6:7] = of_own(entry_ref)
     vals[7:8] = of_own(step_ref)
     vals[8:9] = of_own(counts_ref)
-    reals = sum(dot_nt(selector, piece) for piece in split(vals[0:16], 3))
+    reals = sum(dot_nt(selector, piece) for piece in split(vals[...], 3))
 
     columns = [halves(reals[0:CAP, j : j + 1]) for j in range(9)]
     step_d, count_d = columns[7], columns[8]
@@ -155,9 +217,9 @@
     win[0:FEATS] = w_in_ref[...].astype(F32)
     w_in = win[...].T.astype(BF16)
     w_mid = w_mid_ref[...]
-    w_out = w_out_ref[...]
+    wout[0:4] = w_out_ref[...].astype(F32)
+    w_out = wout[...].astype(BF16)
     half = one_hot(iota((8, 2 * S), 0) == iota((8, 2 * S), 1) // S)
-    sent = []
     for tile in range(ROWS // TILE):
         span = slice(tile * TILE * 128, (tile + 1) * TILE * 128)
         encoded = jnp.concatenate(
@@ -170,62 +232,46 @@
         two_ref[:, span] = two
         raw = dot(w_out, two)
         for j in range(TILE):
-            raws[pl.ds(tile * TILE + j, 4, stride=ROWS), :] = raw[:, j * 128 : (j + 1) * 128]
-        rows = slice(tile * TILE, (tile + 1) * TILE)
-        raw = [raws[c * ROWS + tile * TILE : c * ROWS + (tile + 1) * TILE] for c in range(4)]
-        scale, optical, entering, weight, albedo = shade(raw, step_d[rows], count_d[rows])
-        sums = jnp.concatenate([weight * albedo[0], weight * albedo[1], weight * albedo[2], -optical], axis=0)
-        sent.append(sum(dot_nt(half, piece) for piece in split(sums, 2)))
-        kept = [entering, weight, scale / (1.0 + jnp.exp(-raw[0]))] + albedo
-        kept = kept + [weight * a * (1.0 - a) for a in albedo]
-        for i, value in enumerate(kept):
-            shade_ref[i * ROWS + tile * TILE : i * ROWS + (tile + 1) * TILE] = value
-    sent = jnp.concatenate(sent, axis=1)
+            raws[pl.ds(tile * TILE + j, 4, stride=ROWS), :] = raw[0:4, j * 128 : (j + 1) * 128]
+    raw = [raws[c * ROWS : (c + 1) * ROWS] for c in range(4)]
+    scale, optical, entering, weight, albedo = shade(raw, step_d, count_d)
+    sums = jnp.concatenate([weight * albedo[0], weight * albedo[1], weight * albedo[2], -optical], axis=0)
+    sent = sum(dot_nt(half, piece) for piece in split(sums, 2))
     send_ref[...] = jnp.broadcast_to(sent[None, 0:2], send_ref.shape)
-
-    zone = iota((ZONES, RG), 0)
-    names = [zone == crossing[k : k + 1] for k in range(K)]
-    ranks[...] = dot(one_hot(names[0] | names[1] | names[2] | names[3]), earlier)
-    place_all = ranks[...]
-    ints[0:4] = crossing.astype(F32)
-    for k in range(K):
-        ints[4 + k : 5 + k] = jnp.sum(jnp.where(names[k], place_all, 0.0), axis=0, keepdims=True)
-    ints[8:9] = (ray // (RG // NB)).astype(F32)
-    ints[9:10] = jnp.ones((1, RG), F32)
-    whole = ints[...].astype(BF16)
-    table = dot_nt(selector, whole)
-    info_ref[0:16] = dot_nt(whole, selector)
-    info_ref[16:24] = sum(dot_nt(piece, selector) for piece in split(vals[16:24], 3))
-    bundle = one_hot(table[:, 8:9].astype(jnp.int32) == iota((SEL, NB), 1))
-    order = dot(bundle, order_ref[0].astype(F32).astype(BF16))
-    lane = iota((SEL, ZONES), 1)
-    lister = ((2 * lane + FIRST) & (ZONES - 1)) + jnp.where(lane < ZONES // 2, part & 1, 1 - (part & 1))
-    lister = lister.astype(F32)
-    positions = iota((8, ZONES), 1).astype(F32).astype(BF16)
-    for k in range(K):
-        named = table[:, k : k + 1]
-        place = table[:, 4 + k : 5 + k].astype(jnp.int32)
-        pick_ref[k * SEL : (k + 1) * SEL] = one_hot(named == lister)
-        wanted = ((lane & 15) == (place & 15)) & ((lane >> 6) == ((place >> 4) & 1))
-        low_ref[k * SEL : (k + 1) * SEL] = (wanted & (place < ROWS)).astype(F32)
-        high_ref[k * SEL : (k + 1) * SEL] = (wanted & (place >= ROWS)).astype(F32)
-        info_ref[24 + k : 25 + k] = dot_nt(positions, one_hot(order == named))[0:1]
-    info_ref[28:32] = jnp.zeros((4, SEL), F32)
-    wout[0:4] = w_out.astype(F32)
-    w_out_t_ref[...] = wout[...].T.astype(BF16)
-    w_mid_t_ref[...] = w_mid.astype(F32).T.astype(BF16)
+    kept = [entering, weight, scale / (1.0 + jnp.exp(-raw[0]))] + albedo + [weight * a * (1.0 - a) for a in albedo]
+    for i, value in enumerate(kept):
+        shade_ref[i * ROWS : (i + 1) * ROWS] = value
+
+    @pl.when(part < EARLY)
+    def _():
+        prepare(
+            part, crossing_ref, target_ref, order_ref, lists_ref, w_mid_ref, w_out_ref,
+            pick_ref, low_ref, high_ref, info_ref, w_mid_t_ref, w_out_t_ref, ints, goals, ranks, wout,
+        )
 
 
 def backward_kernel(
-    part_ref, near_ref, other_ref, pick_ref, low_ref, high_ref, info_ref, shade_ref, enc_ref, one_ref, two_ref,
-    w_mid_t_ref, w_out_t_ref,
-    rendered_ref, grads_ref,
-    draw,
+    part_ref, near_ref, other_ref, enc_ref, one_ref, two_ref, shade_ref,
+    crossing_ref, target_ref, order_ref, lists_ref, w_mid_ref, w_out_ref, *refs,
 ):
+    ready, (rendered_ref, grads_ref), work, (draw, *room) = refs[0:6], refs[6:8], refs[8:14], refs[14:]
+    pick_ref, low_ref, high_ref, info_ref, w_mid_t_ref, w_out_t_ref = work
+
+    @pl.when(part_ref[0] < EARLY)
+    def _():
+        for source, target in zip(ready, work):
+            target[...] = source[...]
+
+    @pl.when(part_ref[0] >= EARLY)
+    def _():
+        prepare(
+            part_ref[0], crossing_ref, target_ref, order_ref, lists_ref, w_mid_ref, w_out_ref, *work, *room
+        )
+
     part = part_ref[0].astype(F32)
     got = [jnp.concatenate([near_ref[:, h, :], other_ref[:, h, :]], axis=0) for h in range(2)]
     pieces = split(jnp.concatenate(got, axis=1), 2)
-    gather = one_hot(iota((8, ZONES), 0) == ((iota((8, ZONES), 1) >> 4) & 3))
+    gather = one_hot(iota((8, ZONES), 0) == iota((8, ZONES), 1) // ROWS)
     pick = pick_ref[...]
     low, high = low_ref[...] > 0.5, high_ref[...] > 0.5
     values = jnp.zeros((8, K * SEL), F32)
@@ -317,9 +363,25 @@
     scalar = pl.BlockSpec(memory_space=pltpu.SMEM)
     params = pltpu.CompilerParams(vmem_limit_bytes=40 * 1024 * 1024)
     shape = jax.ShapeDtypeStruct
+    listed = listing()
+    lists = jnp.asarray(np.array([listed[0] + listed[1], listed[1] + listed[0]], np.float32))
     arguments = [in_hbm(a) for a in (
-        anchor, direct, entry, step, counts, crossing, target, order, w_in_t, w_mid[0], w_out[0]
+        anchor, direct, entry, step, counts, crossing, target, order, w_in_t, w_mid[0], w_out[0], lists
     )]
+    prepared = (
+        shape((K * SEL, ZONES), BF16),
+        shape((K * SEL, ZONES), F32),
+        shape((K * SEL, ZONES), F32),
+        shape((32, SEL), F32),
+        shape((256, 256), BF16),
+        shape((256, 16), BF16),
+    )
+    room = [
+        pltpu.VMEM((16, RG), F32),
+        pltpu.VMEM((8, RG), F32),
+        pltpu.VMEM((ZONES, RG), F32),
+        pltpu.VMEM((16, 256), F32),
+    ]
     send, *kept = pl.pallas_call(
         forward_kernel,
         out_shape=(
@@ -327,43 +389,35 @@
             shape((64, COLS), BF16),
             shape((256, COLS), BF16),
             shape((256, COLS), BF16),
-            shape((K * SEL, ZONES), BF16),
-            shape((K * SEL, ZONES), F32),
-            shape((K * SEL, ZONES), F32),
-            shape((32, SEL), F32),
             shape((9 * ROWS, 128), F32),
-            shape((256, 256), BF16),
-            shape((256, 16), BF16),
+            *(shape(a.shape, a.dtype) for a in (crossing, target, order, lists, w_mid[0], w_out[0])),
+            *prepared,
         ),
-        in_specs=[scalar] + [pl.BlockSpec(memory_space=pltpu.HBM)] * 11,
-        out_specs=vmem(11),
-        scratch_shapes=[pltpu.VMEM(a.shape, a.dtype) for a in arguments]
+        in_specs=[scalar] + [pl.BlockSpec(memory_space=pltpu.HBM)] * len(arguments),
+        out_specs=vmem(17),
+        scratch_shapes=[pltpu.VMEM(a.shape, a.dtype) for a in (anchor, direct, entry, step, counts, w_in_t)]
         + [
-            pltpu.VMEM((24, RG), F32),
             pltpu.VMEM((16, RG), F32),
-            pltpu.VMEM((ZONES, RG), F32),
             pltpu.VMEM((64 * ROWS, 128), F32),
             pltpu.VMEM((4 * ROWS, 128), F32),
             pltpu.VMEM((64, 256), F32),
-            pltpu.VMEM((16, 256), F32),
-            pltpu.SemaphoreType.DMA((11,)),
+            *room,
+            pltpu.SemaphoreType.DMA((len(arguments),)),
         ],
         compiler_params=params,
         name="forward",
     )(part, *arguments)
-    listed = [[(2 * i + FIRST) % ZONES + core for i in range(ZONES // 2)] for core in range(2)]
     near = lax.all_to_all(send, "dom", 0, 0, axis_index_groups=listed)
     other = lax.ppermute(near, "dom", [(i, i ^ 1) for i in range(ZONES)])
-    enc, one, two, pick, low, high, info, shaded, w_mid_t, w_out_t = kept
     rendered, grads = pl.pallas_call(
         backward_kernel,
         out_shape=(shape((3, 1, OWN), F32), shape((4, CHUNK, 256), F32)),
-        in_specs=[scalar] + vmem(12),
+        in_specs=[scalar] + vmem(2 + len(kept)),
         out_specs=vmem(2),
-        scratch_shapes=[pltpu.VMEM((16 * ROWS, 128), F32)],
+        scratch_shapes=[pltpu.VMEM(a.shape, a.dtype) for a in prepared] + [pltpu.VMEM((16 * ROWS, 128), F32), *room],
         compiler_params=params,
         name="backward",
-    )(part, near, other, pick, low, high, info, shaded, enc, one, two, w_mid_t, w_out_t)
+    )(part, near, other, *kept)
     shares = lax.all_to_all(grads, "ray", 0, 0, axis_index_groups=[[2, 1, 0, 3]])
     total = jnp.sum(shares, axis=0)
     everything = lax.all_to_all(jnp.broadcast_to(total[None], grads.shape), "ray", 0, 0, axis_index_groups=[[2, 1, 0, 3]])

time: 60.2 us -> 59 us (0.980)
  blocking collectives: 46.4 us -> 45 us
    all_to_all x1, blocking collectives: 25.6 us -> 24.1 us  [local(): near = lax.all_to_all(send, 'dom', 0, 0, axis_index_groups=listed)]
where the time goes in v5:
time: 59 us; the launch traced here: 58.4 us
  blocking collectives  45 us (76%)
  Pallas kernels  9.61 us (16%)
  starting transfers between devices  1.91 us (3%)
  waiting for transfers between devices  1.22 us (2%)
  between operations  0.68 us (1%)
    all_to_all x1, blocking collectives, local(): near = lax.all_to_all(send, 'dom', 0, 0, axis_index_groups=listed)  24.1 us
    all_to_all x1, blocking collectives, local(): lax.all_to_all(grads, 'ray', 0, 0, axis_index_groups=[[2, 1, 0, 3]])  10.9 us
    all_to_all x1, blocking collectives, local(): lax.all_to_all(jnp.broadcast_to(total[None], grads.shape), 'ray', 0, 0, a...  9.87 us
    pallas_call x1, Pallas kernels, local(): pl.pallas_call(forward_kernel, out_shape=(shape((ZONES // 2, 2, 128), F32...  4.82 us
    pallas_call x1, Pallas kernels, local(): pl.pallas_call(backward_kernel, out_shape=(shape((3, 1, OWN), F32), shape...  4.06 us
    ppermute x1, starting transfers between devices, local(): other = lax.ppermute(near, 'dom', [(i, i ^ 1) for i in range(ZONES)])  1.91 us
    ppermute x1, waiting for transfers between devices, local(): other = lax.ppermute(near, 'dom', [(i, i ^ 1) for i in range(ZONES)])  1.22 us
  transfers between devices with their start and end apart: 1, of which 1 were waited for; matrix products, arithmetic and copies ran while one was open for 0% of the time, Pallas kernels for 0%

profile of v5, /device:TPU:6, one launch (start us, length us, event | category | flops | bytes accessed | tf_op | source)
XLA Modules:
  0.0 58.4 jit_solution(17867276480870775827)
XLA Ops:
  0.6 4.8 %forward.1 = (f32[64,2,128]{2,1,0:T(2,128)S(1)}, bf16[64,4096]{1,0:T(8,128)(2,1)S(1)}, bf16[256,4096]{1,0:T(8,128)(2,1)S(1)}, bf16[256,4096]{1,0:T(8,128)(2,1)S(...) custom-call(s32[1]{0:T(128)} %bitcast.part_ref, ...), custom_call_target="tpu_custom_call" | custom-call | tf_op jit(solution)/shard_map/forward/pallas_call | solution.py:385
  5.5 24.1 %all_to_all.15.near_ref = f32[64,2,128]{2,1,0:T(2,128)S(1)} all-to-all(f32[64,2,128]{2,1,0:T(2,128)S(1)} %get-tuple-element.26), channel_id=1, replica_groups={{336,64,32,72,88,96,0,40,56,80,104,120,128,8,24,48,112,136,152,160,480,..., dimensions={0} | all-to-all | bytes 131072 | tf_op jit(solution)/shard_map/all_to_all | solution.py:410
  29.6 1.9 %collective-permute-start = (f32[64,2,128]{2,1,0:T(2,128)S(1)}, f32[64,2,128]{2,1,0:T(2,128)S(1)}, u32[]{:S(2)}, u32[]{:S(2)}) collective-permute-start(f32[64,2,128]{2,1,0:T(2,128)S(1)} %all_to_all.15.near_ref), channel_id=1, source_target_pairs={{0,4},{4,0},{8,12},{12,8},{16,20},{20,16},{24,28},{28,24},{32,36},... | collective-permute-start | bytes 196616 | tf_op jit(solution)/shard_map/ppermute | solution.py:411
  31.5 1.2 %collective-permute-done.other_ref = f32[64,2,128]{2,1,0:T(2,128)S(1)} collective-permute-done((f32[64,2,128]{2,1,0:T(2,128)S(1)}, f32[64,2,128]{2,1,0:T(2,128)S(1)}, u32[]{:S(2)}, u32[]{:S(2)}) %collective-permute-start) | collective-permute-done | bytes 65568 | tf_op jit(solution)/shard_map/ppermute | solution.py:411
  32.7 4.1 %backward.1 = (f32[3,1,4]{2,1,0:T(1,128)}, f32[4,88,256]{2,1,0:T(8,128)S(1)}) custom-call(s32[1]{0:T(128)} %bitcast.part_ref, f32[64,2,128]{2,1,0:T(2,128)S(1)} %all_to_all.15.near_ref, f32[64,2,128]{2,1,0:T(2,128)S(1)} %collective-permute-done.other_ref, bf16[64,4096]{1,0:T(8,128)(2,1)S(1)} %get-tuple-element.27.enc_ref, ...), custom_call_target="tpu_custom_call" | custom-call | tf_op jit(solution)/shard_map/backward/pallas_call | solution.py:412
  36.8 10.9 %all_to_all.16 = f32[4,88,256]{2,1,0:T(8,128)S(1)} all-to-all(f32[4,88,256]{2,1,0:T(8,128)S(1)} %get-tuple-element.44), channel_id=1, replica_groups={{2,1,0,3},{6,5,4,7},{10,9,8,11},{14,13,12,15},{18,17,16,19},{22,21,20,2..., dimensions={0} | all-to-all | bytes 720896 | tf_op jit(solution)/shard_map/all_to_all | solution.py:421
  47.8 9.9 %all_to_all.17.all_ref = f32[4,88,256]{2,1,0:T(8,128)S(1)} all-to-all(f32[4,88,256]{2,1,0:T(8,128)S(1)} %broadcast_in_dim.12), channel_id=1, replica_groups={{2,1,0,3},{6,5,4,7},{10,9,8,11},{14,13,12,15},{18,17,16,19},{22,21,20,2..., dimensions={0} | all-to-all | bytes 720896 | tf_op jit(solution)/shard_map/all_to_all | solution.py:423
  57.7 0.7 %unpack.1 = (f32[63,1,256]{2,1,0:T(1,128)}, f32[256,256]{1,0:T(8,128)}, f32[4,256]{1,0:T(4,128)}) custom-call(f32[4,88,256]{2,1,0:T(8,128)S(1)} %all_to_all.17.all_ref), custom_call_target="tpu_custom_call" | custom-call | tf_op jit(solution)/shard_map/unpack/pallas_call | solution.py:424
  (2 shorter events, 0.0 us)
Async XLA Ops:
  29.6 3.1 %collective-permute-start = (f32[64,2,128]{2,1,0:T(2,128)S(1)}, f32[64,2,128]{2,1,0:T(2,128)S(1)}, u32[]{:S(2)}, u32[]{:S(2)}) collective-permute-start(f32[64,2,128]{2,1,0:T(2,128)S(1)} %all_to_all.15.near_ref), channel_id=1, source_target_pairs={{0,4},{4,0},{8,12},{12,8},{16,20},{20,16},{24,28},{28,24},{32,36},... | collective-permute-start | bytes 196616 | tf_op jit(solution)/shard_map/ppermute | solution.py:411

commit v6 on v5

--- a/solution.py
+++ b/solution.py
@@ -24,7 +24,7 @@
 SPAN = (16, 4)
 COLS = CAP * S
 TILE = 16
-CHUNK = 88
+CHUNK = 168
 F32 = jnp.float32
 BF16 = jnp.bfloat16
 
@@ -335,17 +335,21 @@
         grad_in = grad_in + dot_nt(d_one, enc_ref[:, span])
     grad_in = grad_in.T
     for q in range(4):
-        grads_ref[q, 0:64] = grad_mid[64 * q : 64 * q + 64]
-        grads_ref[q, 64:80] = grad_in[16 * q : 16 * q + 16]
-        grads_ref[q, 80:88] = jnp.broadcast_to(grad_out[q : q + 1], (8, 256))
+        for h in range(2):
+            half = slice(128 * h, 128 * h + 128)
+            grads_ref[q, 64 * h : 64 * h + 64] = grad_mid[64 * q : 64 * q + 64, half]
+            grads_ref[q, 128 + 16 * h : 144 + 16 * h] = grad_in[16 * q : 16 * q + 16, half]
+            grads_ref[q, 160 + 4 * h : 164 + 4 * h] = jnp.broadcast_to(grad_out[q : q + 1, half], (4, 128))
 
 
 def unpack_kernel(all_ref, in_ref, mid_ref, out_ref):
     for q in range(4):
-        mid_ref[64 * q : 64 * q + 64] = all_ref[q, 0:64]
         rows = min(16, FEATS - 16 * q)
-        in_ref[16 * q : 16 * q + rows, 0, :] = all_ref[q, 64 : 64 + rows]
-        out_ref[q : q + 1] = all_ref[q, 80:81]
+        for h in range(2):
+            half = slice(128 * h, 128 * h + 128)
+            mid_ref[64 * q : 64 * q + 64, half] = all_ref[q, 64 * h : 64 * h + 64]
+            in_ref[16 * q : 16 * q + rows, 0, half] = all_ref[q, 128 + 16 * h : 128 + 16 * h + rows]
+            out_ref[q : q + 1, half] = all_ref[q, 160 + 4 * h : 161 + 4 * h]
 
 
 def vmem(count):
@@ -411,7 +415,7 @@
     other = lax.ppermute(near, "dom", [(i, i ^ 1) for i in range(ZONES)])
     rendered, grads = pl.pallas_call(
         backward_kernel,
-        out_shape=(shape((3, 1, OWN), F32), shape((4, CHUNK, 256), F32)),
+        out_shape=(shape((3, 1, OWN), F32), shape((4, CHUNK, 128), F32)),
         in_specs=[scalar] + vmem(2 + len(kept)),
         out_specs=vmem(2),
         scratch_shapes=[pltpu.VMEM(a.shape, a.dtype) for a in prepared] + [pltpu.VMEM((16 * ROWS, 128), F32), *room],

time: 59 us -> 58.5 us (level)
  blocking collectives: 45 us -> 44.4 us
where the time goes in v6:
time: 58.5 us; the launch traced here: 57.9 us
  blocking collectives  44.4 us (76%)
  Pallas kernels  9.61 us (16%)
  starting transfers between devices  1.91 us (3%)
  waiting for transfers between devices  1.22 us (2%)
  between operations  0.67 us (1%)
    all_to_all x1, blocking collectives, local(): near = lax.all_to_all(send, 'dom', 0, 0, axis_index_groups=listed)  24.1 us
    all_to_all x1, blocking collectives, local(): lax.all_to_all(grads, 'ray', 0, 0, axis_index_groups=[[2, 1, 0, 3]])  10.8 us
    all_to_all x1, blocking collectives, local(): lax.all_to_all(jnp.broadcast_to(total[None], grads.shape), 'ray', 0, 0, a...  9.5 us
    pallas_call x1, Pallas kernels, local(): pl.pallas_call(forward_kernel, out_shape=(shape((ZONES // 2, 2, 128), F32...  4.81 us
    pallas_call x1, Pallas kernels, local(): pl.pallas_call(backward_kernel, out_shape=(shape((3, 1, OWN), F32), shape...  4.06 us
    ppermute x1, starting transfers between devices, local(): other = lax.ppermute(near, 'dom', [(i, i ^ 1) for i in range(ZONES)])  1.91 us
    ppermute x1, waiting for transfers between devices, local(): other = lax.ppermute(near, 'dom', [(i, i ^ 1) for i in range(ZONES)])  1.22 us
  transfers between devices with their start and end apart: 1, of which 1 were waited for; matrix products, arithmetic and copies ran while one was open for 0% of the time, Pallas kernels for 0%

profile of v6, /device:TPU:6, one launch (start us, length us, event | category | flops | bytes accessed | tf_op | source)
XLA Modules:
  0.0 57.9 jit_solution(9175026111221092033)
XLA Ops:
  0.6 4.8 %forward.1 = (f32[64,2,128]{2,1,0:T(2,128)S(1)}, bf16[64,4096]{1,0:T(8,128)(2,1)S(1)}, bf16[256,4096]{1,0:T(8,128)(2,1)S(1)}, bf16[256,4096]{1,0:T(8,128)(2,1)S(...) custom-call(s32[1]{0:T(128)} %bitcast.part_ref, ...), custom_call_target="tpu_custom_call" | custom-call | tf_op jit(solution)/shard_map/forward/pallas_call | solution.py:389
  5.5 24.1 %all_to_all.15.near_ref = f32[64,2,128]{2,1,0:T(2,128)S(1)} all-to-all(f32[64,2,128]{2,1,0:T(2,128)S(1)} %get-tuple-element.26), channel_id=1, replica_groups={{336,64,32,72,88,96,0,40,56,80,104,120,128,8,24,48,112,136,152,160,480,..., dimensions={0} | all-to-all | bytes 131072 | tf_op jit(solution)/shard_map/all_to_all | solution.py:414
  29.6 1.9 %collective-permute-start = (f32[64,2,128]{2,1,0:T(2,128)S(1)}, f32[64,2,128]{2,1,0:T(2,128)S(1)}, u32[]{:S(2)}, u32[]{:S(2)}) collective-permute-start(f32[64,2,128]{2,1,0:T(2,128)S(1)} %all_to_all.15.near_ref), channel_id=1, source_target_pairs={{0,4},{4,0},{8,12},{12,8},{16,20},{20,16},{24,28},{28,24},{32,36},... | collective-permute-start | bytes 196616 | tf_op jit(solution)/shard_map/ppermute | solution.py:415
  31.5 1.2 %collective-permute-done.other_ref = f32[64,2,128]{2,1,0:T(2,128)S(1)} collective-permute-done((f32[64,2,128]{2,1,0:T(2,128)S(1)}, f32[64,2,128]{2,1,0:T(2,128)S(1)}, u32[]{:S(2)}, u32[]{:S(2)}) %collective-permute-start) | collective-permute-done | bytes 65568 | tf_op jit(solution)/shard_map/ppermute | solution.py:415
  32.7 4.1 %backward.1 = (f32[3,1,4]{2,1,0:T(1,128)}, f32[4,168,128]{2,1,0:T(8,128)S(1)}) custom-call(s32[1]{0:T(128)} %bitcast.part_ref, f32[64,2,128]{2,1,0:T(2,128)S(1)} %all_to_all.15.near_ref, f32[64,2,128]{2,1,0:T(2,128)S(1)} %collective-permute-done.other_ref, bf16[64,4096]{1,0:T(8,128)(2,1)S(1)} %get-tuple-element.27.enc_ref, ...), custom_call_target="tpu_custom_call" | custom-call | tf_op jit(solution)/shard_map/backward/pallas_call | solution.py:416
  36.8 10.8 %all_to_all.16 = f32[4,168,128]{2,1,0:T(8,128)S(1)} all-to-all(f32[4,168,128]{2,1,0:T(8,128)S(1)} %get-tuple-element.44), channel_id=1, replica_groups={{2,1,0,3},{6,5,4,7},{10,9,8,11},{14,13,12,15},{18,17,16,19},{22,21,20,2..., dimensions={0} | all-to-all | bytes 688128 | tf_op jit(solution)/shard_map/all_to_all | solution.py:425
  47.6 9.5 %all_to_all.17.all_ref = f32[4,168,128]{2,1,0:T(8,128)S(1)} all-to-all(f32[4,168,128]{2,1,0:T(8,128)S(1)} %broadcast_in_dim.12), channel_id=1, replica_groups={{2,1,0,3},{6,5,4,7},{10,9,8,11},{14,13,12,15},{18,17,16,19},{22,21,20,2..., dimensions={0} | all-to-all | bytes 688128 | tf_op jit(solution)/shard_map/all_to_all | solution.py:427
  57.1 0.7 %unpack.1 = (f32[63,1,256]{2,1,0:T(1,128)}, f32[256,256]{1,0:T(8,128)}, f32[4,256]{1,0:T(4,128)}) custom-call(f32[4,168,128]{2,1,0:T(8,128)S(1)} %all_to_all.17.all_ref), custom_call_target="tpu_custom_call" | custom-call | tf_op jit(solution)/shard_map/unpack/pallas_call | solution.py:428
  (2 shorter events, 0.0 us)
Async XLA Ops:
  29.6 3.1 %collective-permute-start = (f32[64,2,128]{2,1,0:T(2,128)S(1)}, f32[64,2,128]{2,1,0:T(2,128)S(1)}, u32[]{:S(2)}, u32[]{:S(2)}) collective-permute-start(f32[64,2,128]{2,1,0:T(2,128)S(1)} %all_to_all.15.near_ref), channel_id=1, source_target_pairs={{0,4},{4,0},{8,12},{12,8},{16,20},{20,16},{24,28},{28,24},{32,36},... | collective-permute-start | bytes 196616 | tf_op jit(solution)/shard_map/ppermute | solution.py:415

commit v7 on v6

--- a/solution.py
+++ b/solution.py
@@ -63,8 +63,8 @@
     return lax.dot_general(a, b, (((1,), (1,)), ((), ())), preferred_element_type=F32)
 
 
-def split_dot(x, exact):
-    return sum(dot(part, exact) for part in split(x, 2))
+def split_dot(x, exact, terms):
+    return sum(dot(part, exact) for part in split(x, terms))
 
 
 def halves(column):
@@ -94,10 +94,10 @@
     density = jnp.maximum(raw[0], 0.0) + jnp.log1p(decay)
     optical = density * scale
     source, target = iota((2 * S, 2 * S), 0), iota((2 * S, 2 * S), 1)
-    upto = one_hot((source <= target) & ((source < S) == (target < S)))
-    reached = split_dot(optical, upto)
-    entering = jnp.exp(optical - reached)
-    weight = entering - jnp.exp(-reached)
+    ahead = one_hot((source < target) & ((source < S) == (target < S)))
+    passed = split_dot(optical, ahead, 2)
+    entering = jnp.exp(-passed)
+    weight = entering - jnp.exp(-(passed + optical))
     albedo = [1.0 / (1.0 + jnp.exp(-raw[c])) for c in (1, 2, 3)]
     return scale, optical, entering, weight, albedo
 
@@ -311,11 +311,11 @@
     gain = sum(dcolor_d[c] * rest[c] for c in range(3))
     source, target = iota((2 * S, 2 * S), 0), iota((2 * S, 2 * S), 1)
     since = one_hot((source >= target) & ((source < S) == (target < S)))
-    behind = split_dot(gain * weight, since)
+    behind = split_dot(gain * weight, since, 3)
     draw[0:ROWS] = (gain * entering - behind - halves(slots[0:CAP, 3:4])) * slope
     for c in range(3):
         draw[(c + 1) * ROWS : (c + 2) * ROWS] = dcolor_d[c] * rest[3 + c]
-    draw[4 * ROWS :] = jnp.zeros((12 * ROWS, 2 * S), F32)
+    draw[4 * ROWS : 16 * ROWS] = jnp.zeros((12 * ROWS, 2 * S), F32)
 
     w_out_t, w_mid_t = w_out_t_ref[...], w_mid_t_ref[...]
     grad_out = jnp.zeros((16, 256), F32)
@@ -402,8 +402,8 @@
         scratch_shapes=[pltpu.VMEM(a.shape, a.dtype) for a in (anchor, direct, entry, step, counts, w_in_t)]
         + [
             pltpu.VMEM((16, RG), F32),
-            pltpu.VMEM((64 * ROWS, 128), F32),
-            pltpu.VMEM((4 * ROWS, 128), F32),
+            pltpu.VMEM((65 * ROWS, 128), F32),
+            pltpu.VMEM((5 * ROWS, 128), F32),
             pltpu.VMEM((64, 256), F32),
             *room,
             pltpu.SemaphoreType.DMA((len(arguments),)),
@@ -418,7 +418,7 @@
         out_shape=(shape((3, 1, OWN), F32), shape((4, CHUNK, 128), F32)),
         in_specs=[scalar] + vmem(2 + len(kept)),
         out_specs=vmem(2),
-        scratch_shapes=[pltpu.VMEM(a.shape, a.dtype) for a in prepared] + [pltpu.VMEM((16 * ROWS, 128), F32), *room],
+        scratch_shapes=[pltpu.VMEM(a.shape, a.dtype) for a in prepared] + [pltpu.VMEM((17 * ROWS, 128), F32), *room],
         compiler_params=params,
         name="backward",
     )(part, near, other, *kept)

time: 58.5 us -> 58.5 us (level)
  no operation moved by 1% of the time
where the time goes in v7:
time: 58.5 us; the launch traced here: 57.9 us
  blocking collectives  44.4 us (76%)
  Pallas kernels  9.65 us (16%)
  starting transfers between devices  1.91 us (3%)
  waiting for transfers between devices  1.22 us (2%)
  between operations  0.67 us (1%)
    all_to_all x1, blocking collectives, local(): near = lax.all_to_all(send, 'dom', 0, 0, axis_index_groups=listed)  24.1 us
    all_to_all x1, blocking collectives, local(): lax.all_to_all(grads, 'ray', 0, 0, axis_index_groups=[[2, 1, 0, 3]])  10.8 us
    all_to_all x1, blocking collectives, local(): lax.all_to_all(jnp.broadcast_to(total[None], grads.shape), 'ray', 0, 0, a...  9.5 us
    pallas_call x1, Pallas kernels, local(): pl.pallas_call(forward_kernel, out_shape=(shape((ZONES // 2, 2, 128), F32...  4.81 us
    pallas_call x1, Pallas kernels, local(): pl.pallas_call(backward_kernel, out_shape=(shape((3, 1, OWN), F32), shape...  4.1 us
    ppermute x1, starting transfers between devices, local(): other = lax.ppermute(near, 'dom', [(i, i ^ 1) for i in range(ZONES)])  1.91 us
    ppermute x1, waiting for transfers between devices, local(): other = lax.ppermute(near, 'dom', [(i, i ^ 1) for i in range(ZONES)])  1.22 us
  transfers between devices with their start and end apart: 1, of which 1 were waited for; matrix products, arithmetic and copies ran while one was open for 0% of the time, Pallas kernels for 0%

profile of v7, /device:TPU:6, one launch (start us, length us, event | category | flops | bytes accessed | tf_op | source)
XLA Modules:
  0.0 57.9 jit_solution(8327265948838571804)
XLA Ops:
  0.6 4.8 %forward.1 = (f32[64,2,128]{2,1,0:T(2,128)S(1)}, bf16[64,4096]{1,0:T(8,128)(2,1)S(1)}, bf16[256,4096]{1,0:T(8,128)(2,1)S(1)}, bf16[256,4096]{1,0:T(8,128)(2,1)S(...) custom-call(s32[1]{0:T(128)} %bitcast.part_ref, ...), custom_call_target="tpu_custom_call" | custom-call | tf_op jit(solution)/shard_map/forward/pallas_call | solution.py:389
  5.5 24.1 %all_to_all.15.near_ref = f32[64,2,128]{2,1,0:T(2,128)S(1)} all-to-all(f32[64,2,128]{2,1,0:T(2,128)S(1)} %get-tuple-element.26), channel_id=1, replica_groups={{336,64,32,72,88,96,0,40,56,80,104,120,128,8,24,48,112,136,152,160,480,..., dimensions={0} | all-to-all | bytes 131072 | tf_op jit(solution)/shard_map/all_to_all | solution.py:414
  29.6 1.9 %collective-permute-start = (f32[64,2,128]{2,1,0:T(2,128)S(1)}, f32[64,2,128]{2,1,0:T(2,128)S(1)}, u32[]{:S(2)}, u32[]{:S(2)}) collective-permute-start(f32[64,2,128]{2,1,0:T(2,128)S(1)} %all_to_all.15.near_ref), channel_id=1, source_target_pairs={{0,4},{4,0},{8,12},{12,8},{16,20},{20,16},{24,28},{28,24},{32,36},... | collective-permute-start | bytes 196616 | tf_op jit(solution)/shard_map/ppermute | solution.py:415
  31.5 1.2 %collective-permute-done.other_ref = f32[64,2,128]{2,1,0:T(2,128)S(1)} collective-permute-done((f32[64,2,128]{2,1,0:T(2,128)S(1)}, f32[64,2,128]{2,1,0:T(2,128)S(1)}, u32[]{:S(2)}, u32[]{:S(2)}) %collective-permute-start) | collective-permute-done | bytes 65568 | tf_op jit(solution)/shard_map/ppermute | solution.py:415
  32.7 4.1 %backward.1 = (f32[3,1,4]{2,1,0:T(1,128)}, f32[4,168,128]{2,1,0:T(8,128)S(1)}) custom-call(s32[1]{0:T(128)} %bitcast.part_ref, f32[64,2,128]{2,1,0:T(2,128)S(1)} %all_to_all.15.near_ref, f32[64,2,128]{2,1,0:T(2,128)S(1)} %collective-permute-done.other_ref, bf16[64,4096]{1,0:T(8,128)(2,1)S(1)} %get-tuple-element.27.enc_ref, ...), custom_call_target="tpu_custom_call" | custom-call | tf_op jit(solution)/shard_map/backward/pallas_call | solution.py:416
  36.8 10.8 %all_to_all.16 = f32[4,168,128]{2,1,0:T(8,128)S(1)} all-to-all(f32[4,168,128]{2,1,0:T(8,128)S(1)} %get-tuple-element.44), channel_id=1, replica_groups={{2,1,0,3},{6,5,4,7},{10,9,8,11},{14,13,12,15},{18,17,16,19},{22,21,20,2..., dimensions={0} | all-to-all | bytes 688128 | tf_op jit(solution)/shard_map/all_to_all | solution.py:425
  47.7 9.5 %all_to_all.17.all_ref = f32[4,168,128]{2,1,0:T(8,128)S(1)} all-to-all(f32[4,168,128]{2,1,0:T(8,128)S(1)} %broadcast_in_dim.12), channel_id=1, replica_groups={{2,1,0,3},{6,5,4,7},{10,9,8,11},{14,13,12,15},{18,17,16,19},{22,21,20,2..., dimensions={0} | all-to-all | bytes 688128 | tf_op jit(solution)/shard_map/all_to_all | solution.py:427
  57.2 0.7 %unpack.1 = (f32[63,1,256]{2,1,0:T(1,128)}, f32[256,256]{1,0:T(8,128)}, f32[4,256]{1,0:T(4,128)}) custom-call(f32[4,168,128]{2,1,0:T(8,128)S(1)} %all_to_all.17.all_ref), custom_call_target="tpu_custom_call" | custom-call | tf_op jit(solution)/shard_map/unpack/pallas_call | solution.py:428
  (2 shorter events, 0.0 us)
Async XLA Ops:
  29.6 3.1 %collective-permute-start = (f32[64,2,128]{2,1,0:T(2,128)S(1)}, f32[64,2,128]{2,1,0:T(2,128)S(1)}, u32[]{:S(2)}, u32[]{:S(2)}) collective-permute-start(f32[64,2,128]{2,1,0:T(2,128)S(1)} %all_to_all.15.near_ref), channel_id=1, source_target_pairs={{0,4},{4,0},{8,12},{12,8},{16,20},{20,16},{24,28},{28,24},{32,36},... | collective-permute-start | bytes 196616 | tf_op jit(solution)/shard_map/ppermute | solution.py:415

commit v8 on v7

--- a/solution.py
+++ b/solution.py
@@ -342,14 +342,26 @@
             grads_ref[q, 160 + 4 * h : 164 + 4 * h] = jnp.broadcast_to(grad_out[q : q + 1, half], (4, 128))
 
 
-def unpack_kernel(all_ref, in_ref, mid_ref, out_ref):
+def unpack_kernel(all_ref, in_ref, mid_hbm, out_ref, sems):
+    copies = [
+        pltpu.make_async_copy(
+            all_ref.at[q, pl.ds(64 * h, 64)],
+            mid_hbm.at[pl.ds(64 * q, 64), pl.ds(128 * h, 128)],
+            sems.at[2 * q + h],
+        )
+        for q in range(4)
+        for h in range(2)
+    ]
+    for copy in copies:
+        copy.start()
     for q in range(4):
         rows = min(16, FEATS - 16 * q)
         for h in range(2):
             half = slice(128 * h, 128 * h + 128)
-            mid_ref[64 * q : 64 * q + 64, half] = all_ref[q, 64 * h : 64 * h + 64]
             in_ref[16 * q : 16 * q + rows, 0, half] = all_ref[q, 128 + 16 * h : 128 + 16 * h + rows]
             out_ref[q : q + 1, half] = all_ref[q, 160 + 4 * h : 161 + 4 * h]
+    for copy in copies:
+        copy.wait()
 
 
 def vmem(count):
@@ -429,7 +441,8 @@
         unpack_kernel,
         out_shape=(shape((FEATS, 1, 256), F32), shape((256, 256), F32), shape((4, 256), F32)),
         in_specs=vmem(1),
-        out_specs=vmem(3),
+        out_specs=[*vmem(1), pl.BlockSpec(memory_space=pltpu.HBM), *vmem(1)],
+        scratch_shapes=[pltpu.SemaphoreType.DMA((8,))],
         compiler_params=params,
         name="unpack",
     )(everything)

time: 58.5 us -> 59.2 us (1.012)
  Pallas kernels: 9.65 us -> 10.3 us
    pallas_call x1, Pallas kernels: 0.74 us -> 1.39 us  [local(): pl.pallas_call(unpack_kernel, out_shape=(shape((FEATS, 1, 256), F32), sha...]
where the time goes in v8:
time: 59.2 us; the launch traced here: 58.5 us
  blocking collectives  44.4 us (75%)
  Pallas kernels  10.3 us (17%)
  starting transfers between devices  1.91 us (3%)
  waiting for transfers between devices  1.22 us (2%)
  between operations  0.67 us (1%)
    all_to_all x1, blocking collectives, local(): near = lax.all_to_all(send, 'dom', 0, 0, axis_index_groups=listed)  24.1 us
    all_to_all x1, blocking collectives, local(): lax.all_to_all(grads, 'ray', 0, 0, axis_index_groups=[[2, 1, 0, 3]])  10.8 us
    all_to_all x1, blocking collectives, local(): lax.all_to_all(jnp.broadcast_to(total[None], grads.shape), 'ray', 0, 0, a...  9.5 us
    pallas_call x1, Pallas kernels, local(): pl.pallas_call(forward_kernel, out_shape=(shape((ZONES // 2, 2, 128), F32...  4.81 us
    pallas_call x1, Pallas kernels, local(): pl.pallas_call(backward_kernel, out_shape=(shape((3, 1, OWN), F32), shape...  4.1 us
    ppermute x1, starting transfers between devices, local(): other = lax.ppermute(near, 'dom', [(i, i ^ 1) for i in range(ZONES)])  1.91 us
    pallas_call x1, Pallas kernels, local(): pl.pallas_call(unpack_kernel, out_shape=(shape((FEATS, 1, 256), F32), sha...  1.39 us
    ppermute x1, waiting for transfers between devices, local(): other = lax.ppermute(near, 'dom', [(i, i ^ 1) for i in range(ZONES)])  1.22 us
  transfers between devices with their start and end apart: 1, of which 1 were waited for; matrix products, arithmetic and copies ran while one was open for 0% of the time, Pallas kernels for 0%

profile of v8, /device:TPU:6, one launch (start us, length us, event | category | flops | bytes accessed | tf_op | source)
XLA Modules:
  0.0 58.5 jit_solution(7006279494104968966)
XLA Ops:
  0.6 4.8 %forward.1 = (f32[64,2,128]{2,1,0:T(2,128)S(1)}, bf16[64,4096]{1,0:T(8,128)(2,1)S(1)}, bf16[256,4096]{1,0:T(8,128)(2,1)S(1)}, bf16[256,4096]{1,0:T(8,128)(2,1)S(...) custom-call(s32[1]{0:T(128)} %bitcast.part_ref, ...), custom_call_target="tpu_custom_call" | custom-call | tf_op jit(solution)/shard_map/forward/pallas_call | solution.py:401
  5.5 24.1 %all_to_all.15.near_ref = f32[64,2,128]{2,1,0:T(2,128)S(1)} all-to-all(f32[64,2,128]{2,1,0:T(2,128)S(1)} %get-tuple-element.26), channel_id=1, replica_groups={{336,64,32,72,88,96,0,40,56,80,104,120,128,8,24,48,112,136,152,160,480,..., dimensions={0} | all-to-all | bytes 131072 | tf_op jit(solution)/shard_map/all_to_all | solution.py:426
  29.6 1.9 %collective-permute-start = (f32[64,2,128]{2,1,0:T(2,128)S(1)}, f32[64,2,128]{2,1,0:T(2,128)S(1)}, u32[]{:S(2)}, u32[]{:S(2)}) collective-permute-start(f32[64,2,128]{2,1,0:T(2,128)S(1)} %all_to_all.15.near_ref), channel_id=1, source_target_pairs={{0,4},{4,0},{8,12},{12,8},{16,20},{20,16},{24,28},{28,24},{32,36},... | collective-permute-start | bytes 196616 | tf_op jit(solution)/shard_map/ppermute | solution.py:427
  31.5 1.2 %collective-permute-done.other_ref = f32[64,2,128]{2,1,0:T(2,128)S(1)} collective-permute-done((f32[64,2,128]{2,1,0:T(2,128)S(1)}, f32[64,2,128]{2,1,0:T(2,128)S(1)}, u32[]{:S(2)}, u32[]{:S(2)}) %collective-permute-start) | collective-permute-done | bytes 65568 | tf_op jit(solution)/shard_map/ppermute | solution.py:427
  32.7 4.1 %backward.1 = (f32[3,1,4]{2,1,0:T(1,128)}, f32[4,168,128]{2,1,0:T(8,128)S(1)}) custom-call(s32[1]{0:T(128)} %bitcast.part_ref, f32[64,2,128]{2,1,0:T(2,128)S(1)} %all_to_all.15.near_ref, f32[64,2,128]{2,1,0:T(2,128)S(1)} %collective-permute-done.other_ref, bf16[64,4096]{1,0:T(8,128)(2,1)S(1)} %get-tuple-element.27.enc_ref, ...), custom_call_target="tpu_custom_call" | custom-call | tf_op jit(solution)/shard_map/backward/pallas_call | solution.py:428
  36.8 10.8 %all_to_all.16 = f32[4,168,128]{2,1,0:T(8,128)S(1)} all-to-all(f32[4,168,128]{2,1,0:T(8,128)S(1)} %get-tuple-element.44), channel_id=1, replica_groups={{2,1,0,3},{6,5,4,7},{10,9,8,11},{14,13,12,15},{18,17,16,19},{22,21,20,2..., dimensions={0} | all-to-all | bytes 688128 | tf_op jit(solution)/shard_map/all_to_all | solution.py:437
  47.7 9.5 %all_to_all.17.all_ref = f32[4,168,128]{2,1,0:T(8,128)S(1)} all-to-all(f32[4,168,128]{2,1,0:T(8,128)S(1)} %broadcast_in_dim.12), channel_id=1, replica_groups={{2,1,0,3},{6,5,4,7},{10,9,8,11},{14,13,12,15},{18,17,16,19},{22,21,20,2..., dimensions={0} | all-to-all | bytes 688128 | tf_op jit(solution)/shard_map/all_to_all | solution.py:439
  57.2 1.4 %unpack.1 = (f32[63,1,256]{2,1,0:T(1,128)}, f32[256,256]{1,0:T(8,128)}, f32[4,256]{1,0:T(4,128)}) custom-call(f32[4,168,128]{2,1,0:T(8,128)S(1)} %all_to_all.17.all_ref), custom_call_target="tpu_custom_call" | custom-call | tf_op jit(solution)/shard_map/unpack/pallas_call | solution.py:440
  (2 shorter events, 0.0 us)
Async XLA Ops:
  29.6 3.1 %collective-permute-start = (f32[64,2,128]{2,1,0:T(2,128)S(1)}, f32[64,2,128]{2,1,0:T(2,128)S(1)}, u32[]{:S(2)}, u32[]{:S(2)}) collective-permute-start(f32[64,2,128]{2,1,0:T(2,128)S(1)} %all_to_all.15.near_ref), channel_id=1, source_target_pairs={{0,4},{4,0},{8,12},{12,8},{16,20},{20,16},{24,28},{28,24},{32,36},... | collective-permute-start | bytes 196616 | tf_op jit(solution)/shard_map/ppermute | solution.py:427

commit v9 on v7

--- a/solution.py
+++ b/solution.py
@@ -19,7 +19,7 @@
 OWN = 4
 ROWS = 32
 SEL = 72
-FIRST = 84
+FIRST = 92
 EARLY = 48
 SPAN = (16, 4)
 COLS = CAP * S

time: 58.5 us -> 58.7 us (level)
  no operation moved by 1% of the time
where the time goes in v9:
time: 58.7 us; the launch traced here: 58.2 us
  blocking collectives  44.7 us (76%)
  Pallas kernels  9.66 us (16%)
  starting transfers between devices  1.91 us (3%)
  waiting for transfers between devices  1.22 us (2%)
  between operations  0.67 us (1%)
    all_to_all x1, blocking collectives, local(): near = lax.all_to_all(send, 'dom', 0, 0, axis_index_groups=listed)  24.4 us
    all_to_all x1, blocking collectives, local(): lax.all_to_all(grads, 'ray', 0, 0, axis_index_groups=[[2, 1, 0, 3]])  10.8 us
    all_to_all x1, blocking collectives, local(): lax.all_to_all(jnp.broadcast_to(total[None], grads.shape), 'ray', 0, 0, a...  9.5 us
    pallas_call x1, Pallas kernels, local(): pl.pallas_call(forward_kernel, out_shape=(shape((ZONES // 2, 2, 128), F32...  4.81 us
    pallas_call x1, Pallas kernels, local(): pl.pallas_call(backward_kernel, out_shape=(shape((3, 1, OWN), F32), shape...  4.1 us
    ppermute x1, starting transfers between devices, local(): other = lax.ppermute(near, 'dom', [(i, i ^ 1) for i in range(ZONES)])  1.91 us
    ppermute x1, waiting for transfers between devices, local(): other = lax.ppermute(near, 'dom', [(i, i ^ 1) for i in range(ZONES)])  1.22 us
  transfers between devices with their start and end apart: 1, of which 1 were waited for; matrix products, arithmetic and copies ran while one was open for 0% of the time, Pallas kernels for 0%

profile of v9, /device:TPU:6, one launch (start us, length us, event | category | flops | bytes accessed | tf_op | source)
XLA Modules:
  0.0 58.2 jit_solution(17650477483782420366)
XLA Ops:
  0.6 4.8 %forward.1 = (f32[64,2,128]{2,1,0:T(2,128)S(1)}, bf16[64,4096]{1,0:T(8,128)(2,1)S(1)}, bf16[256,4096]{1,0:T(8,128)(2,1)S(1)}, bf16[256,4096]{1,0:T(8,128)(2,1)S(...) custom-call(s32[1]{0:T(128)} %bitcast.part_ref, ...), custom_call_target="tpu_custom_call" | custom-call | tf_op jit(solution)/shard_map/forward/pallas_call | solution.py:389
  5.5 24.4 %all_to_all.15.near_ref = f32[64,2,128]{2,1,0:T(2,128)S(1)} all-to-all(f32[64,2,128]{2,1,0:T(2,128)S(1)} %get-tuple-element.26), channel_id=1, replica_groups={{368,96,64,104,120,128,32,72,88,112,136,152,160,0,40,56,80,144,168,184,..., dimensions={0} | all-to-all | bytes 131072 | tf_op jit(solution)/shard_map/all_to_all | solution.py:414
  29.9 1.9 %collective-permute-start = (f32[64,2,128]{2,1,0:T(2,128)S(1)}, f32[64,2,128]{2,1,0:T(2,128)S(1)}, u32[]{:S(2)}, u32[]{:S(2)}) collective-permute-start(f32[64,2,128]{2,1,0:T(2,128)S(1)} %all_to_all.15.near_ref), channel_id=1, source_target_pairs={{0,4},{4,0},{8,12},{12,8},{16,20},{20,16},{24,28},{28,24},{32,36},... | collective-permute-start | bytes 196616 | tf_op jit(solution)/shard_map/ppermute | solution.py:415
  31.8 1.2 %collective-permute-done.other_ref = f32[64,2,128]{2,1,0:T(2,128)S(1)} collective-permute-done((f32[64,2,128]{2,1,0:T(2,128)S(1)}, f32[64,2,128]{2,1,0:T(2,128)S(1)}, u32[]{:S(2)}, u32[]{:S(2)}) %collective-permute-start) | collective-permute-done | bytes 65568 | tf_op jit(solution)/shard_map/ppermute | solution.py:415
  33.0 4.1 %backward.1 = (f32[3,1,4]{2,1,0:T(1,128)}, f32[4,168,128]{2,1,0:T(8,128)S(1)}) custom-call(s32[1]{0:T(128)} %bitcast.part_ref, f32[64,2,128]{2,1,0:T(2,128)S(1)} %all_to_all.15.near_ref, f32[64,2,128]{2,1,0:T(2,128)S(1)} %collective-permute-done.other_ref, bf16[64,4096]{1,0:T(8,128)(2,1)S(1)} %get-tuple-element.27.enc_ref, ...), custom_call_target="tpu_custom_call" | custom-call | tf_op jit(solution)/shard_map/backward/pallas_call | solution.py:416
  37.1 10.8 %all_to_all.16 = f32[4,168,128]{2,1,0:T(8,128)S(1)} all-to-all(f32[4,168,128]{2,1,0:T(8,128)S(1)} %get-tuple-element.44), channel_id=1, replica_groups={{2,1,0,3},{6,5,4,7},{10,9,8,11},{14,13,12,15},{18,17,16,19},{22,21,20,2..., dimensions={0} | all-to-all | bytes 688128 | tf_op jit(solution)/shard_map/all_to_all | solution.py:425
  48.0 9.5 %all_to_all.17.all_ref = f32[4,168,128]{2,1,0:T(8,128)S(1)} all-to-all(f32[4,168,128]{2,1,0:T(8,128)S(1)} %broadcast_in_dim.12), channel_id=1, replica_groups={{2,1,0,3},{6,5,4,7},{10,9,8,11},{14,13,12,15},{18,17,16,19},{22,21,20,2..., dimensions={0} | all-to-all | bytes 688128 | tf_op jit(solution)/shard_map/all_to_all | solution.py:427
  57.5 0.7 %unpack.1 = (f32[63,1,256]{2,1,0:T(1,128)}, f32[256,256]{1,0:T(8,128)}, f32[4,256]{1,0:T(4,128)}) custom-call(f32[4,168,128]{2,1,0:T(8,128)S(1)} %all_to_all.17.all_ref), custom_call_target="tpu_custom_call" | custom-call | tf_op jit(solution)/shard_map/unpack/pallas_call | solution.py:428
  (2 shorter events, 0.0 us)
Async XLA Ops:
  29.9 3.1 %collective-permute-start = (f32[64,2,128]{2,1,0:T(2,128)S(1)}, f32[64,2,128]{2,1,0:T(2,128)S(1)}, u32[]{:S(2)}, u32[]{:S(2)}) collective-permute-start(f32[64,2,128]{2,1,0:T(2,128)S(1)} %all_to_all.15.near_ref), channel_id=1, source_target_pairs={{0,4},{4,0},{8,12},{12,8},{16,20},{20,16},{24,28},{28,24},{32,36},... | collective-permute-start | bytes 196616 | tf_op jit(solution)/shard_map/ppermute | solution.py:415
